TPU v7x, 32 devices: a whole 2x2x4 slice. The times are simulated.
32 devices in a mesh: tm: 4 (over x, core), chan: 8 (over z, y).
Axes of the slice: x: 2, y: 2, z: 4, core: 2. Of those that a mesh axis runs over, the one named last changes fastest.
Arguments:
- voltages: float32 [512, 262144], P('chan', 'tm'), may hold values from -6 to 6
- fir_taps: float32 [4, 2048], replicated, may hold values from -3 to 3
Outputs:
- visibilities: float32 [1024, 2, 512, 512], P(('tm', 'chan'))
All inputs are finite; a program needn't handle non-finite values.
Results may differ from a plain program's by a relative error of at most 0.00009.
Values sent between devices are 32-bit elements; how exact they have to be, the bound alone decides.
No kernel may reach another device: no remote copies, remote signals or barrier semaphores. Data moves between devices by JAX's collectives and lax.ppermute only.
A program may use at most 192 MiB of HBM per device.

v0:
```python
import jax
import jax.numpy as jnp
from jax import lax
from jax.sharding import PartitionSpec as P


def passed_along(value, axis, steps):
    count = lax.axis_size(axis)
    first, last = (max(0, -steps), min(count, count - steps))
    return lax.ppermute(value, axis, [(source, source + steps) for source in range(first, last)])


def dft_table(frame):
    rows = lax.broadcasted_iota(jnp.int32, (frame, frame), 0)
    cols = lax.broadcasted_iota(jnp.int32, (frame, frame), 1)
    channel = rows // 2
    part = rows % 2
    phase = (channel * cols % frame).astype(jnp.float32) * (2.0 * jnp.pi / frame)
    scale = 1.0 / jnp.sqrt(jnp.float32(frame))
    return jnp.where(part == 0, jnp.cos(phase), -jnp.sin(phase)) * scale


def correlate(owned):
    spectra_count = owned.shape[3]
    stacked = jnp.concatenate([owned[:, 0], owned[:, 1]], axis=2)
    turned = jnp.concatenate([owned[:, 1], -owned[:, 0]], axis=2)
    both = jnp.concatenate([stacked, turned], axis=1)
    gram = jnp.einsum("cps,cqs->cpq", both, stacked, precision=lax.Precision.HIGHEST) * (
        1.0 / spectra_count
    )
    return gram.reshape(owned.shape[0], 2, owned.shape[2], owned.shape[2])


def body(voltages, fir_taps):
    inp_dev = voltages.shape[0]
    frame = fir_taps.shape[1]
    spec_dev = voltages.shape[1] // frame
    edge = fir_taps.shape[0] - 1
    frames = voltages.reshape(inp_dev, spec_dev, frame)
    earlier = passed_along(frames[:, spec_dev - edge :, :], "tm", 1)
    extended = jnp.concatenate([earlier, frames], axis=1)
    filtered = fir_taps[0] * frames
    for tap in range(1, edge + 1):
        filtered = filtered + fir_taps[tap] * extended[:, edge - tap : edge - tap + spec_dev, :]
    table = dft_table(frame)
    spectra = jnp.einsum("kn,isn->kis", table, filtered, precision=lax.Precision.HIGHEST)
    spectra = spectra.reshape(frame // 2, 2, inp_dev, spec_dev)
    tm_count = lax.axis_size("tm")
    chan_count = lax.axis_size("chan")
    moved = lax.all_to_all(spectra[None], ("tm", "chan"), split_axis=1, concat_axis=0, tiled=True)
    owned_count = moved.shape[1]
    moved = moved.reshape(tm_count, chan_count, owned_count, 2, inp_dev, spec_dev)
    moved = jnp.transpose(moved, (2, 3, 1, 4, 0, 5))
    owned = moved.reshape(owned_count, 2, chan_count * inp_dev, tm_count * spec_dev)
    return correlate(owned)


def solution(mesh):
    placed = (P("chan", "tm"), P())
    return jax.shard_map(
        body,
        mesh=mesh,
        in_specs=placed,
        out_specs=P(("tm", "chan"), None, None, None),
        check_vma=False,
    )
```

profile of v0, /device:TPU:0, one launch (start us, length us, event | category | flops | bytes accessed | tf_op | source)
XLA Modules:
  0.0 953.9 jit_solution(1938546478774115723)
XLA Ops:
  0.0 0.0 slice-start
  0.0 0.0 copy-start.1
  0.0 0.0 slice-start.1
  0.0 0.0 slice-start.2
  0.0 0.0 slice-start.3
  0.0 7.3 copy.37
  7.3 0.1 slice.42
  7.4 2.9 collective-permute-start
  10.4 0.0 copy-done.1
  10.4 2.8 collective-permute-done
  13.2 0.1 constant_dynamic-update-slice_fusion.1
  13.4 0.0 slice-done
  13.4 0.0 slice-done.1
  13.4 0.0 slice-done.2
  13.4 0.0 slice-done.3
  13.4 2.2 constant_dynamic-update-slice_fusion
  15.7 0.0 copy-start
  15.7 6.7 copy-done
  22.4 29.3 %fusion.75 = f32[64,32,2048]{2,0,1:T(8,128)} fusion(f32[64,35,2048]{2,0,1:T(8,128)} %copy-done, f32[2048]{0:T(1024)S(1)} %bitcast.54, f32[2048]{0:T(1024)S(1)} %bitcast.55, f32[2048]{0:T(1024)S(1)} %bitcast.53, f32[2048]{0:T(1024)S(1)} %bitcast.52, f32[8,32,8,2048]{3,2,1,0:T(8,128)} %bitcast.42), kind=kLoop, calls=%fused_computation.18.clone.clone.2 | loop fusion | flops 29360128 | bytes 83918848 | tf_op jit(solution)/shard_map/kn,isn->kis/dot_general | solution.py:46
  51.7 191.0 %fusion.14 = f32[2048,64,32]{0,1,2:T(8,128)} fusion(s32[2048]{0:T(1024)S(1)} %get-tuple-element.11, s32[2048]{0:T(1024)S(1)} %get-tuple-element.14, s32[2048]{0:T(1024)S(1)} %get-tuple-element.12, s32[2048]{0:T(1024)S(1)} %get-tuple-element.13, pred[2048]{0:T(1024)(128)(4,1)S(1)} %get-tuple-element.15, pred[2048]{0:T(1024)(128)(4,1)S(1)} %get-tuple-element.16, ...), kind=kOutput, calls=%fused_computation.19 | convolution fusion | flops 103163101184 | bytes 33591296 | tf_op jit(solution)/shard_map/kn,isn->kis/dot_general | solution.py:46
  242.7 30.4 %copy.17 = f32[2048,64,32]{1,2,0:T(8,128)} copy(f32[2048,64,32]{0,1,2:T(8,128)} %fusion.14) | data formatting | bytes 33554432 | tf_op jit(solution)/shard_map/kn,isn->kis/dot_general | solution.py:46
  273.1 35.6 %reshape.25 = f32[32,1,131072]{2,1,0:T(1,128)} reshape(f32[1024,1,2,32,64]{4,3,2,1,0:T(8,128)} %bitcast.46) | data formatting | bytes 33554432
  308.7 388.3 %all_to_all.4 = f32[32,1,131072]{2,1,0:T(1,128)} all-to-all(f32[32,1,131072]{2,1,0:T(1,128)} %reshape.25), channel_id=1, replica_groups=mesh['tm'=4,'chan'=8] {'tm','chan'}, dimensions={0} | all-to-all | bytes 33554432 | tf_op jit(solution)/shard_map/all_to_all | solution.py:50
  697.0 0.5 broadcast.37
  697.5 47.9 %reduce = f32[32,131072]{1,0:T(8,128)} reduce(f32[32,1,131072]{2,1,0:T(1,128)} %all_to_all.4, f32[]{:T(128)} %broadcast.37), dimensions={1}, to_apply=%all_to_all.2.reduce_sub_computation | reduce | bytes 33554436 | tf_op jit(solution)/shard_map/all_to_all | solution.py:50
  745.4 35.4 %reshape.26 = f32[1024,1,2,32,64]{4,3,2,1,0:T(8,128)} reshape(f32[32,131072]{1,0:T(8,128)} %reduce) | data formatting | bytes 33554432
  780.9 37.9 %copy.36 = f32[4,8,32,2,64,32]{4,1,5,0,3,2:T(8,128)} copy(f32[4,8,32,2,64,32]{4,5,3,2,1,0:T(8,128)} %bitcast.47) | data formatting | bytes 33554432 | tf_op jit(solution)/shard_map/reshape | solution.py:52
  818.8 27.6 %reshape.22 = f32[32,2,512,128]{2,3,1,0:T(8,128)} reshape(f32[32,2,8,64,4,32]{3,2,5,4,1,0:T(8,128)} %bitcast.48) | data formatting | bytes 33554432 | tf_op jit(solution)/shard_map/reshape | solution.py:54
  846.4 10.7 %fusion.61 = (f32[32,1,512,128]{2,3,1,0:T(8,128)}, f32[32,1,512,128]{2,3,1,0:T(8,128)}) fusion(f32[32,2,512,128]{2,3,1,0:T(8,128)} %reshape.22), kind=kLoop, calls=%fused_computation.72 | loop fusion | bytes 33554432 | tf_op jit(solution)/shard_map/slice | solution.py:25
  857.2 9.0 copy.23
  866.2 9.0 copy.22
  875.1 7.5 bitcast_negate_fusion
  882.7 71.2 %broadcast_multiply_fusion = f32[32,1024,512]{2,1,0:T(8,128)} fusion(f32[32,512,128]{2,1,0:T(8,128)} %bitcast_negate_fusion, f32[32,512,128]{2,1,0:T(8,128)} %bitcast.51, f32[32,512,128]{2,1,0:T(8,128)} %bitcast.49), kind=kOutput, calls=%fused_computation.9 | convolution fusion | flops 51585744896 | bytes 92274688 | tf_op jit(solution)/shard_map/cps,cqs->cpq/dot_general | solution.py:28
  (5 shorter events, 0.0 us)
Async XLA Ops:
  0.0 13.4 %slice-start = ((s8[16777216]{0:T(1024)(128)(4,1)}), s8[4194304]{0:T(1024)(128)(4,1)S(1)}, s32[]{:S(2)}) async-start(s8[16777216]{0:T(1024)(128)(4,1)} %bitcast.43), calls=%async_computation.1 | async-start | bytes 8388608
  0.0 10.4 %copy-start.1 = (f32[4,2048]{1,0:T(4,128)S(1)}, f32[4,2048]{1,0:T(4,128)}, u32[]{:S(2)}) copy-start(f32[4,2048]{1,0:T(4,128)} %param.3) | copy-start | bytes 98308
  0.0 13.4 %slice-start.1 = ((s8[16777216]{0:T(1024)(128)(4,1)}), s8[4194304]{0:T(1024)(128)(4,1)S(1)}, s32[]{:S(2)}) async-start(s8[16777216]{0:T(1024)(128)(4,1)} %bitcast.43), calls=%async_computation.2 | async-start | bytes 8388608
  0.0 13.4 %slice-start.2 = ((s8[16777216]{0:T(1024)(128)(4,1)}), s8[4194304]{0:T(1024)(128)(4,1)S(1)}, s32[]{:S(2)}) async-start(s8[16777216]{0:T(1024)(128)(4,1)} %bitcast.43), calls=%async_computation.3 | async-start | bytes 8388608
  0.0 13.4 %slice-start.3 = ((s8[16777216]{0:T(1024)(128)(4,1)}), s8[4194304]{0:T(1024)(128)(4,1)S(1)}, s32[]{:S(2)}) async-start(s8[16777216]{0:T(1024)(128)(4,1)} %bitcast.43), calls=%async_computation.4 | async-start | bytes 8388608
  7.4 5.8 collective-permute-start
  15.7 6.7 copy-start
where the time goes:
time: 957 us; the launch traced here: 954 us
  blocking collectives  388 us (41%)
  matrix products  262 us (27%)
  local copies, waits for them, and re-layouts  213 us (22%)
  other arithmetic  84.8 us (9%)
    all_to_all x1, blocking collectives, body(): lax.all_to_all(spectra[None], ('tm', 'chan'), split_axis=1, concat_axis=0...  388 us
    dot_general x1, matrix products, body(): jnp.einsum('kn,isn->kis', table, filtered, precision=lax.Precision.HIGHEST)  191 us
    unnamed x17, local copies, waits for them, and re-layouts  95.9 us
    dot_general x1, matrix products, correlate(): jnp.einsum('cps,cqs->cpq', both, stacked, precision=lax.Precision.HIGHEST)  71.2 us
    all_to_all x1, other arithmetic, body(): lax.all_to_all(spectra[None], ('tm', 'chan'), split_axis=1, concat_axis=0...  47.9 us
    reshape x1, local copies, waits for them, and re-layouts, body(): moved.reshape(tm_count, chan_count, owned_count, 2, inp_dev, spec_dev)  37.9 us
    dot_general x1, local copies, waits for them, and re-layouts, body(): jnp.einsum('kn,isn->kis', table, filtered, precision=lax.Precision.HIGHEST)  30.4 us
    dot_general x1, other arithmetic, body(): jnp.einsum('kn,isn->kis', table, filtered, precision=lax.Precision.HIGHEST)  29.3 us
  transfers between devices with their start and end apart: 1, of which 1 were waited for; matrix products, arithmetic and copies ran while one was open for 0% of the time, Pallas kernels for 0%

commit v1 on v0

v1 whole, which is shorter than its diff:
```python
import functools

import jax
import jax.numpy as jnp
import numpy as np
from jax import lax
from jax.experimental import pallas as pl
from jax.experimental.pallas import tpu as pltpu
from jax.sharding import PartitionSpec as P

LANES = 128
AXES = ("tm", "chan")
NT = (((1,), (1,)), ((), ()))
NN = (((1,), (0,)), ((), ()))


def params(mib):
    return pltpu.CompilerParams(vmem_limit_bytes=mib << 20)


def halves(value):
    high = value.astype(jnp.bfloat16)
    low = (value - high.astype(jnp.float32)).astype(jnp.bfloat16)
    return high, low


def passed_along(value, axis, steps):
    count = lax.axis_size(axis)
    first, last = (max(0, -steps), min(count, count - steps))
    return lax.ppermute(value, axis, [(source, source + steps) for source in range(first, last)])


def filter_kernel(blocks, groups, taps, volt_ref, halo_ref, fir_ref, high_ref, low_ref):
    frame = fir_ref.shape[1]
    edge = taps - 1

    def put(spec, terms):
        total = terms[0] * fir_ref[0:1, :]
        for tap in range(1, taps):
            total = total + terms[tap] * fir_ref[tap : tap + 1, :]
        high, low = halves(total)
        at = (lax.rem(spec, blocks), lax.div(spec, blocks))
        high_ref[at] = high
        low_ref[at] = low

    def old(spec):
        if spec < 0:
            return halo_ref[:, (spec + edge) * frame : (spec + edge + 1) * frame]
        return volt_ref[:, spec * frame : (spec + 1) * frame]

    for spec in range(edge):
        put(spec, [old(spec - tap) for tap in range(taps)])

    def step(spec, carry):
        put(
            spec,
            [
                volt_ref[:, pl.ds(pl.multiple_of((spec - tap) * frame, frame), frame)]
                for tap in range(taps)
            ],
        )
        return carry

    lax.fori_loop(edge, blocks * groups, step, 0)


def filtered_parts(voltages, halo, fir_taps, blocks, groups):
    inputs, samples = voltages.shape
    taps, frame = fir_taps.shape
    rows = 16
    shape = jax.ShapeDtypeStruct((blocks, groups, inputs, frame), jnp.bfloat16)
    out_spec = pl.BlockSpec((blocks, groups, rows, frame), lambda g: (0, 0, g, 0))
    high, low = pl.pallas_call(
        functools.partial(filter_kernel, blocks, groups, taps),
        grid=(inputs // rows,),
        in_specs=[
            pl.BlockSpec((rows, samples), lambda g: (g, 0)),
            pl.BlockSpec((rows, halo.shape[1]), lambda g: (g, 0)),
            pl.BlockSpec((taps, frame), lambda g: (0, 0)),
        ],
        out_specs=[out_spec, out_spec],
        out_shape=[shape, shape],
        compiler_params=params(40),
        cost_estimate=pl.CostEstimate(
            flops=8 * inputs * samples, bytes_accessed=8 * inputs * samples, transcendentals=0
        ),
        name="polyphase_filter",
    )(voltages, halo, fir_taps)
    rows_all = blocks * groups * inputs
    return high.reshape(rows_all, frame), low.reshape(rows_all, frame)


def dft_kernel(owners, per, outer_ref, first_ref, second_ref, high_ref, low_ref, out_ref, th_ref, tl_ref):
    many = max(1, 16 // per)
    frame = high_ref.shape[1]

    @pl.when(pl.program_id(0) == 0)
    def _():
        def rows(step, carry):
            parts = []
            for extra in range(many):
                owner = step * many + extra
                cosine = outer_ref[0, pl.ds(owner, 1), :]
                sine = outer_ref[1, pl.ds(owner, 1), :]
                parts.append(first_ref[...] * cosine + second_ref[...] * sine)
            value = parts[0] if many == 1 else jnp.concatenate(parts, axis=0)
            high, low = halves(value)
            at = pl.ds(pl.multiple_of(step * many * per, many * per), many * per)
            th_ref[at, :] = high
            tl_ref[at, :] = low
            return carry

        lax.fori_loop(0, owners // many, rows, 0)

    dot = functools.partial(lax.dot_general, dimension_numbers=NT, preferred_element_type=jnp.float32)
    total = dot(th_ref[...], high_ref[...])
    total = total + dot(th_ref[...], low_ref[...])
    total = total + dot(tl_ref[...], high_ref[...])
    for block in range(out_ref.shape[1]):
        part = total[:, block * LANES : (block + 1) * LANES]
        out_ref[:, block] = part.reshape(owners, per, LANES)


def dft_chunk(outer, first, second, high, low, owners, blocks):
    per, frame = first.shape
    wide = 2
    rows = wide * LANES
    const = lambda b: (0, 0)
    return pl.pallas_call(
        functools.partial(dft_kernel, owners, per),
        grid=(blocks // wide,),
        in_specs=[
            pl.BlockSpec((2, owners, frame), lambda b: (0, 0, 0)),
            pl.BlockSpec((per, frame), const),
            pl.BlockSpec((per, frame), const),
            pl.BlockSpec((rows, frame), lambda b: (b, 0)),
            pl.BlockSpec((rows, frame), lambda b: (b, 0)),
        ],
        out_specs=pl.BlockSpec((owners, wide, per, LANES), lambda b: (0, b, 0, 0)),
        out_shape=jax.ShapeDtypeStruct((owners, blocks, per, LANES), jnp.float32),
        scratch_shapes=[
            pltpu.VMEM((owners * per, frame), jnp.bfloat16),
            pltpu.VMEM((owners * per, frame), jnp.bfloat16),
        ],
        compiler_params=params(40),
        cost_estimate=pl.CostEstimate(
            flops=6 * owners * per * frame * blocks * LANES,
            bytes_accessed=4 * blocks * LANES * frame + 4 * owners * blocks * per * LANES,
            transcendentals=0,
        ),
        name="dft_chunk",
    )(outer, first, second, high, low)


def correlate_kernel(sizes, scale, got_ref, *rest):
    tm_count, chan_count, blocks, per, inputs = sizes
    out_ref = rest[-1]
    channel = pl.program_id(0)
    groups = LANES // inputs
    channels = per // 2
    lane_group = lax.broadcasted_iota(jnp.int32, (blocks, LANES), 1) // inputs

    def piece(time, chan, part):
        start = (time * chan_count + chan) * blocks * per + part * channels + channel
        return got_ref[pl.ds(start, blocks, stride=per), :]

    def tile(time, part, column):
        held = [piece(time, column * groups + place, part) for place in range(groups)]
        made = []
        for group in range(groups):
            total = None
            for place in range(groups):
                turn = (place - group) * inputs % LANES
                value = pltpu.roll(held[place], turn, 1) if turn else held[place]
                total = value if total is None else jnp.where(lane_group == place, value, total)
            made.append(total)
        return jnp.concatenate(made, axis=0)

    def plane(part):
        columns = []
        for column in range(chan_count // groups):
            columns.append(
                jnp.concatenate([tile(time, part, column) for time in range(tm_count)], axis=0)
            )
        return jnp.concatenate(columns, axis=1)

    real, imag = plane(0), plane(1)
    real_high, real_low = halves(real)
    imag_high, imag_low = halves(imag)
    high = jnp.concatenate([real_high, imag_high], axis=0)
    low = jnp.concatenate([real_low, imag_low], axis=0)
    turned_high = jnp.concatenate([-imag_high, real_high], axis=0)
    turned_low = jnp.concatenate([-imag_low, real_low], axis=0)
    high_t, low_t = high.T, low.T
    dot = functools.partial(lax.dot_general, dimension_numbers=NN, preferred_element_type=jnp.float32)
    for which, (other_high, other_low) in enumerate([(high, low), (turned_high, turned_low)]):
        total = dot(high_t, other_high) + dot(high_t, other_low) + dot(low_t, other_high)
        out_ref[0, which] = total * scale


def correlate_chunk(got, held, start, owned, sizes, spectra):
    tm_count, chan_count, blocks, per, inputs = sizes
    channels = per // 2
    everyone = chan_count * inputs
    rows = got.shape[0] * got.shape[1] * got.shape[2]
    first = start // channels
    operands = [got.reshape(rows, LANES)]
    in_specs = [pl.BlockSpec((rows, LANES), lambda c: (0, 0))]
    aliases = {}
    if held is not None:
        operands.append(held)
        in_specs.append(pl.BlockSpec(memory_space=pl.ANY))
        aliases = {1: 0}
    return pl.pallas_call(
        functools.partial(correlate_kernel, sizes, 1.0 / spectra),
        grid=(channels,),
        in_specs=in_specs,
        out_specs=pl.BlockSpec((1, 2, everyone, everyone), lambda c: (start + c, 0, 0, 0)),
        out_shape=jax.ShapeDtypeStruct((owned, 2, everyone, everyone), jnp.float32),
        input_output_aliases=aliases,
        compiler_params=params(40),
        cost_estimate=pl.CostEstimate(
            flops=6 * channels * 2 * everyone * everyone * 2 * spectra,
            bytes_accessed=channels * 8 * everyone * everyone + 4 * rows * LANES,
            transcendentals=0,
        ),
        name="correlate_chunk",
    )(*operands)


def phases(frame, owners, owned, chunk):
    samples = np.arange(frame)
    outer = 2.0 * np.pi * ((np.arange(owners)[:, None] * owned * samples) % frame) / frame
    inner = 2.0 * np.pi * ((np.arange(owned)[:, None] * samples) % frame) / frame
    scale = 1.0 / np.sqrt(float(frame))
    cosine, sine = np.cos(inner) * scale, np.sin(inner) * scale
    outer = np.stack([np.cos(outer), np.sin(outer)]).astype(np.float32)
    tables = []
    for start in range(0, owned, chunk):
        here = slice(start, start + chunk)
        first = np.concatenate([cosine[here], -sine[here]]).astype(np.float32)
        second = np.concatenate([-sine[here], -cosine[here]]).astype(np.float32)
        tables.append((start, first, second))
    return outer, tables


def body(voltages, fir_taps):
    inputs, samples = voltages.shape
    taps, frame = fir_taps.shape
    spec_dev = samples // frame
    tm_count, chan_count = lax.axis_size("tm"), lax.axis_size("chan")
    owners = tm_count * chan_count
    owned = frame // 2 // owners
    groups = LANES // inputs
    blocks = spec_dev // groups
    chunk = max(4, owned // 4)
    halo = passed_along(voltages[:, samples - (taps - 1) * frame :], "tm", 1)
    high, low = filtered_parts(voltages, halo, fir_taps, blocks, groups)
    outer, tables = phases(frame, owners, owned, chunk)
    sizes = (tm_count, chan_count, blocks, 2 * chunk, inputs)
    moved = []
    for start, first, second in tables:
        made = dft_chunk(outer, first, second, high, low, owners, blocks)
        moved.append((start, lax.all_to_all(made, AXES, split_axis=0, concat_axis=0, tiled=True)))
    out = None
    for start, got in moved:
        out = correlate_chunk(got, out, start, owned, sizes, tm_count * spec_dev)
    return out


def solution(mesh):
    placed = (P("chan", "tm"), P())
    return jax.shard_map(
        body,
        mesh=mesh,
        in_specs=placed,
        out_specs=P(("tm", "chan"), None, None, None),
        check_vma=False,
    )
```

time: 957 us -> 476 us (0.50)
  blocking collectives: 388 us -> 0 us
  waiting for transfers between devices: 2.84 us -> 277 us
  matrix products: 262 us -> 0 us
  local copies, waits for them, and re-layouts: 213 us -> 23.6 us
  Pallas kernels: 0 us -> 138 us
  other arithmetic: 84.8 us -> 0 us
  starting transfers between devices: 2.87 us -> 37.2 us
    all_to_all x1 -> x0, blocking collectives: 388 us -> none  [body(): lax.all_to_all(spectra[None], ('tm', 'chan'), split_axis=1, concat_axis=0...]
    all_to_all x0 -> x4, waiting for transfers between devices: none -> 274 us  [body(): lax.all_to_all(made, AXES, split_axis=0, concat_axis=0, tiled=True)]
    dot_general x2 -> x0, matrix products: 262 us -> none  [the longest x1 191 us: body(): jnp.einsum('kn,isn->kis', table, filtered, precision=lax.Precision.HIGHEST)]
    pallas_call x0 -> x9, Pallas kernels: none -> 138 us  [the longest x4 69.3 us: dft_chunk(): pl.pallas_call(functools.partial(dft_kernel, owners, per), grid=(blocks /...]
    unnamed x17 -> x36, local copies, waits for them, and re-layouts: 95.9 us -> 22 us
    reshape x3 -> x0, local copies, waits for them, and re-layouts: 72.8 us -> none  [the longest x1 37.9 us: body(): moved.reshape(tm_count, chan_count, owned_count, 2, inp_dev, spec_dev)]
    all_to_all x1 -> x0, other arithmetic: 47.9 us -> none  [body(): lax.all_to_all(spectra[None], ('tm', 'chan'), split_axis=1, concat_axis=0...]
    all_to_all x0 -> x4, starting transfers between devices: none -> 34.7 us  [body(): lax.all_to_all(made, AXES, split_axis=0, concat_axis=0, tiled=True)]
  transfers between devices with their start and end apart: 1 -> 5, of which waited for: 1 -> 5; matrix products, arithmetic and copies ran while one was open for 0% -> 0% of each run, Pallas kernels for 0% -> 20%
where the time goes in v1:
time: 476 us; the launch traced here: 475 us
  waiting for transfers between devices  277 us (58%)
  Pallas kernels  138 us (29%)
  starting transfers between devices  37.2 us (8%)
  local copies, waits for them, and re-layouts  23.6 us (5%)
    all_to_all x4, waiting for transfers between devices, body(): lax.all_to_all(made, AXES, split_axis=0, concat_axis=0, tiled=True)  274 us
    pallas_call x4, Pallas kernels, dft_chunk(): pl.pallas_call(functools.partial(dft_kernel, owners, per), grid=(blocks /...  69.3 us
    pallas_call x4, Pallas kernels, correlate_chunk(): pl.pallas_call(functools.partial(correlate_kernel, sizes, 1.0 / spectra),...  55.6 us
    all_to_all x4, starting transfers between devices, body(): lax.all_to_all(made, AXES, split_axis=0, concat_axis=0, tiled=True)  34.7 us
    unnamed x36, local copies, waits for them, and re-layouts  22 us
    pallas_call x1, Pallas kernels, filtered_parts(): pl.pallas_call(functools.partial(filter_kernel, blocks, groups, taps), gr...  12.7 us
  transfers between devices with their start and end apart: 5, of which 5 were waited for; matrix products, arithmetic and copies ran while one was open for 0% of the time, Pallas kernels for 20%

profile of v1, /device:TPU:0, one launch (start us, length us, event | category | flops | bytes accessed | tf_op | source)
XLA Modules:
  0.0 475.4 jit_solution(6348779595575509773)
XLA Ops:
  0.0 0.0 copy-start.9
  0.0 0.0 copy-start.16
  0.0 0.0 copy-start.17
  0.0 1.6 slice.3
  1.6 2.5 collective-permute-start
  4.1 2.9 collective-permute-done.halo_ref
  7.0 0.8 copy-done.4
  7.8 12.7 %polyphase_filter.1 = (bf16[16,2,64,2048]{3,2,1,0:T(8,128)(2,1)S(1)}, bf16[16,2,64,2048]{3,2,1,0:T(8,128)(2,1)}) custom-call(f32[64,65536]{1,0:T(8,128)} %volt_ref.1, f32[64,6144]{1,0:T(8,128)S(1)} %collective-permute-done.halo_ref, f32[4,2048]{1,0:T(4,128)S(1)} %copy-done.4), custom_call_target="tpu_custom_call" | custom-call | flops 33554432 | bytes 33554432 | tf_op jit(solution)/shard_map/polyphase_filter/pallas_call | solution.py:73
  20.5 0.0 copy-done.9
  20.5 0.0 copy-done.16
  20.5 0.0 copy-done.17
  20.5 17.3 %dft_chunk.7 = f32[32,16,16,128]{3,2,1,0:T(8,128)S(1)} custom-call(f32[2,32,2048]{2,1,0:T(8,128)S(1)} %copy-done.9, f32[16,2048]{1,0:T(8,128)S(1)} %copy-done.17, f32[16,2048]{1,0:T(8,128)S(1)} %copy-done.16, bf16[2048,2048]{1,0:T(8,128)(2,1)S(1)} %bitcast.6, bf16[2048,2048]{1,0:T(8,128)(2,1)} %bitcast.10), custom_call_target="tpu_custom_call" | custom-call | flops 12884901888 | bytes 20971520 | tf_op jit(solution)/shard_map/dft_chunk/pallas_call | solution.py:129
  37.8 0.0 copy-start.3
  37.9 1.9 copy-done.3
  39.8 3.3 copy-done.5
  43.1 23.8 %all-to-all-start.3 = ((f32[32,16,16,128]{3,2,1,0:T(8,128)}), f32[32,16,16,128]{3,2,1,0:T(8,128)}, u32[]{:S(2)}, u32[]{:S(2)}) async-start(f32[32,16,16,128]{3,2,1,0:T(8,128)} %copy-done.3), calls=%async_computation.3 | async-start | bytes 8388608 | tf_op jit(solution)/shard_map/all_to_all | solution.py:264
  66.8 0.0 copy-done.14
  66.9 0.0 copy-done.15
  66.9 0.0 copy-start.6
  66.9 3.4 copy-done.6
  70.3 17.3 %dft_chunk.6 = f32[32,16,16,128]{3,2,1,0:T(8,128)S(1)} custom-call(f32[2,32,2048]{2,1,0:T(8,128)S(1)} %copy-done.9, f32[16,2048]{1,0:T(8,128)S(1)} %copy-done.15, f32[16,2048]{1,0:T(8,128)S(1)} %copy-done.14, bf16[2048,2048]{1,0:T(8,128)(2,1)S(1)} %bitcast.7, bf16[2048,2048]{1,0:T(8,128)(2,1)} %bitcast.11), custom_call_target="tpu_custom_call" | custom-call | flops 12884901888 | bytes 20971520 | tf_op jit(solution)/shard_map/dft_chunk/pallas_call | solution.py:129
  87.6 0.0 copy-start.2
  87.6 1.9 copy-done.2
  89.5 73.3 %all-to-all-done.3 = f32[32,16,16,128]{3,2,1,0:T(8,128)} async-done(((f32[32,16,16,128]{3,2,1,0:T(8,128)}), f32[32,16,16,128]{3,2,1,0:T(8,128)}, u32[]{:S(2)}, u32[]{:S(2)}) %all-to-all-start.3) | async-done | bytes 4194336 | tf_op jit(solution)/shard_map/all_to_all | solution.py:264
  162.8 3.6 all-to-all-start.2
  166.4 0.0 copy-done.12
  166.4 0.0 copy-done.13
  166.4 0.0 copy-start.7
  166.4 3.4 copy-done.7
  169.8 17.3 %dft_chunk.5 = f32[32,16,16,128]{3,2,1,0:T(8,128)S(1)} custom-call(f32[2,32,2048]{2,1,0:T(8,128)S(1)} %copy-done.9, f32[16,2048]{1,0:T(8,128)S(1)} %copy-done.13, f32[16,2048]{1,0:T(8,128)S(1)} %copy-done.12, bf16[2048,2048]{1,0:T(8,128)(2,1)S(1)} %bitcast.8, bf16[2048,2048]{1,0:T(8,128)(2,1)} %bitcast.12), custom_call_target="tpu_custom_call" | custom-call | flops 12884901888 | bytes 20971520 | tf_op jit(solution)/shard_map/dft_chunk/pallas_call | solution.py:129
  187.1 0.0 copy-start.1
  187.2 2.0 copy-done.1
  189.2 73.2 %all-to-all-done.2 = f32[32,16,16,128]{3,2,1,0:T(8,128)} async-done(((f32[32,16,16,128]{3,2,1,0:T(8,128)}), f32[32,16,16,128]{3,2,1,0:T(8,128)}, u32[]{:S(2)}, u32[]{:S(2)}) %all-to-all-start.2) | async-done | bytes 4194336 | tf_op jit(solution)/shard_map/all_to_all | solution.py:264
  262.4 3.6 all-to-all-start.1
  266.0 0.0 copy-done.10
  266.0 0.0 copy-done.11
  266.0 0.0 copy-start.8
  266.0 3.4 copy-done.8
  269.4 17.3 %dft_chunk.4 = f32[32,16,16,128]{3,2,1,0:T(8,128)S(1)} custom-call(f32[2,32,2048]{2,1,0:T(8,128)S(1)} %copy-done.9, f32[16,2048]{1,0:T(8,128)S(1)} %copy-done.11, f32[16,2048]{1,0:T(8,128)S(1)} %copy-done.10, bf16[2048,2048]{1,0:T(8,128)(2,1)S(1)} %bitcast.9, bf16[2048,2048]{1,0:T(8,128)(2,1)} %bitcast.13), custom_call_target="tpu_custom_call" | custom-call | flops 12884901888 | bytes 20971520 | tf_op jit(solution)/shard_map/dft_chunk/pallas_call | solution.py:129
  286.7 0.0 copy-start
  286.7 1.9 copy-done
  288.6 73.3 %all-to-all-done.1 = f32[32,16,16,128]{3,2,1,0:T(8,128)} async-done(((f32[32,16,16,128]{3,2,1,0:T(8,128)}), f32[32,16,16,128]{3,2,1,0:T(8,128)}, u32[]{:S(2)}, u32[]{:S(2)}) %all-to-all-start.1) | async-done | bytes 4194336 | tf_op jit(solution)/shard_map/all_to_all | solution.py:264
  361.9 3.8 all-to-all-start
  365.7 13.9 %correlate_chunk.4.rest_0_ = f32[32,2,512,512]{3,2,1,0:T(8,128)} custom-call(f32[8192,128]{1,0:T(8,128)} %bitcast.5.got_ref), custom_call_target="tpu_custom_call" | custom-call | flops 6442450944 | bytes 20971520 | tf_op jit(solution)/shard_map/correlate_chunk/pallas_call | solution.py:214
  379.6 13.9 %correlate_chunk.5.rest_0_ = f32[32,2,512,512]{3,2,1,0:T(8,128)} custom-call(f32[8192,128]{1,0:T(8,128)} %bitcast.4.got_ref, f32[32,2,512,512]{3,2,1,0:T(8,128)} %correlate_chunk.4.rest_0_), custom_call_target="tpu_custom_call", output_to_operand_aliasing={{}: (1, {})} | custom-call | flops 6442450944 | bytes 20971520 | tf_op jit(solution)/shard_map/correlate_chunk/pallas_call | solution.py:214
  393.5 13.9 %correlate_chunk.6.rest_0_ = f32[32,2,512,512]{3,2,1,0:T(8,128)} custom-call(f32[8192,128]{1,0:T(8,128)} %bitcast.3.got_ref, f32[32,2,512,512]{3,2,1,0:T(8,128)} %correlate_chunk.5.rest_0_), custom_call_target="tpu_custom_call", output_to_operand_aliasing={{}: (1, {})} | custom-call | flops 6442450944 | bytes 20971520 | tf_op jit(solution)/shard_map/correlate_chunk/pallas_call | solution.py:214
  407.4 54.1 %all-to-all-done = f32[32,16,16,128]{3,2,1,0:T(8,128)} async-done(((f32[32,16,16,128]{3,2,1,0:T(8,128)}), f32[32,16,16,128]{3,2,1,0:T(8,128)}, u32[]{:S(2)}, u32[]{:S(2)}) %all-to-all-start) | async-done | bytes 4194336 | tf_op jit(solution)/shard_map/all_to_all | solution.py:264
  461.5 13.9 %correlate_chunk.7 = f32[32,2,512,512]{3,2,1,0:T(8,128)} custom-call(f32[8192,128]{1,0:T(8,128)} %bitcast.2.got_ref, f32[32,2,512,512]{3,2,1,0:T(8,128)} %correlate_chunk.6.rest_0_), custom_call_target="tpu_custom_call", output_to_operand_aliasing={{}: (1, {})} | custom-call | flops 6442450944 | bytes 20971520 | tf_op jit(solution)/shard_map/correlate_chunk/pallas_call | solution.py:214
  (8 shorter events, 0.0 us)
Async XLA Ops:
  0.0 20.5 %copy-start.9 = (f32[2,32,2048]{2,1,0:T(8,128)S(1)}, f32[2,32,2048]{2,1,0:T(8,128)}, u32[]{:S(2)}) copy-start(f32[2,32,2048]{2,1,0:T(8,128)} %constant.18.clone.outer_ref) | copy-start | bytes 1572868
  0.0 20.5 %copy-start.16 = (f32[16,2048]{1,0:T(8,128)S(1)}, f32[16,2048]{1,0:T(8,128)}, u32[]{:S(2)}) copy-start(f32[16,2048]{1,0:T(8,128)} %constant.20.clone.second_ref) | copy-start | bytes 393220
  0.0 20.5 %copy-start.17 = (f32[16,2048]{1,0:T(8,128)S(1)}, f32[16,2048]{1,0:T(8,128)}, u32[]{:S(2)}) copy-start(f32[16,2048]{1,0:T(8,128)} %constant.19.clone.first_ref) | copy-start | bytes 393220
  1.6 5.4 %collective-permute-start = (f32[64,6144]{1,0:T(8,128)S(1)}, f32[64,6144]{1,0:T(8,128)S(1)}, u32[]{:S(2)}, u32[]{:S(2)}) collective-permute-start(f32[64,6144]{1,0:T(8,128)S(1)} %slice.3), channel_id=1, source_target_pairs={{0,8},{8,16},{16,24},{1,9},{9,17},{17,25},{2,10},{10,18},{18,26},{... | collective-permute-start | bytes 4718600 | tf_op jit(solution)/shard_map/ppermute | solution.py:30
  7.0 0.8 copy-start.4
  37.8 1.9 copy-start.3
  39.8 3.3 copy-start.5
  43.1 23.8 %copy-start.14 = (f32[16,2048]{1,0:T(8,128)S(1)}, f32[16,2048]{1,0:T(8,128)}, u32[]{:S(2)}) copy-start(f32[16,2048]{1,0:T(8,128)} %constant.22.clone.second_ref) | copy-start | bytes 393220
  43.1 23.8 %copy-start.15 = (f32[16,2048]{1,0:T(8,128)S(1)}, f32[16,2048]{1,0:T(8,128)}, u32[]{:S(2)}) copy-start(f32[16,2048]{1,0:T(8,128)} %constant.21.clone.first_ref) | copy-start | bytes 393220
  43.1 119.7 %all-to-all-start.3 = ((f32[32,16,16,128]{3,2,1,0:T(8,128)}), f32[32,16,16,128]{3,2,1,0:T(8,128)}, u32[]{:S(2)}, u32[]{:S(2)}) async-start(f32[32,16,16,128]{3,2,1,0:T(8,128)} %copy-done.3), calls=%async_computation.3 | async-start | bytes 8388608 | tf_op jit(solution)/shard_map/all_to_all | solution.py:264
  66.9 3.4 copy-start.6
  87.6 1.9 copy-start.2
  89.5 76.9 %copy-start.12 = (f32[16,2048]{1,0:T(8,128)S(1)}, f32[16,2048]{1,0:T(8,128)}, u32[]{:S(2)}) copy-start(f32[16,2048]{1,0:T(8,128)} %constant.24.clone.second_ref) | copy-start | bytes 393220
  89.5 76.9 %copy-start.13 = (f32[16,2048]{1,0:T(8,128)S(1)}, f32[16,2048]{1,0:T(8,128)}, u32[]{:S(2)}) copy-start(f32[16,2048]{1,0:T(8,128)} %constant.23.clone.first_ref) | copy-start | bytes 393220
  162.8 99.6 %all-to-all-start.2 = ((f32[32,16,16,128]{3,2,1,0:T(8,128)}), f32[32,16,16,128]{3,2,1,0:T(8,128)}, u32[]{:S(2)}, u32[]{:S(2)}) async-start(f32[32,16,16,128]{3,2,1,0:T(8,128)} %copy-done.2), calls=%async_computation.2 | async-start | bytes 8388608 | tf_op jit(solution)/shard_map/all_to_all | solution.py:264
  166.4 3.4 copy-start.7
  187.1 2.0 copy-start.1
  189.2 76.8 %copy-start.10 = (f32[16,2048]{1,0:T(8,128)S(1)}, f32[16,2048]{1,0:T(8,128)}, u32[]{:S(2)}) copy-start(f32[16,2048]{1,0:T(8,128)} %constant.26.clone.second_ref) | copy-start | bytes 393220
  189.2 76.8 %copy-start.11 = (f32[16,2048]{1,0:T(8,128)S(1)}, f32[16,2048]{1,0:T(8,128)}, u32[]{:S(2)}) copy-start(f32[16,2048]{1,0:T(8,128)} %constant.25.clone.first_ref) | copy-start | bytes 393220
  262.4 99.5 %all-to-all-start.1 = ((f32[32,16,16,128]{3,2,1,0:T(8,128)}), f32[32,16,16,128]{3,2,1,0:T(8,128)}, u32[]{:S(2)}, u32[]{:S(2)}) async-start(f32[32,16,16,128]{3,2,1,0:T(8,128)} %copy-done.1), calls=%async_computation.1 | async-start | bytes 8388608 | tf_op jit(solution)/shard_map/all_to_all | solution.py:264
  266.0 3.4 copy-start.8
  286.7 2.0 copy-start
  361.9 99.6 %all-to-all-start = ((f32[32,16,16,128]{3,2,1,0:T(8,128)}), f32[32,16,16,128]{3,2,1,0:T(8,128)}, u32[]{:S(2)}, u32[]{:S(2)}) async-start(f32[32,16,16,128]{3,2,1,0:T(8,128)} %copy-done), calls=%async_computation | async-start | bytes 8388608 | tf_op jit(solution)/shard_map/all_to_all | solution.py:264

commit v2 on v1

--- a/solution.py
+++ b/solution.py
@@ -1,4 +1,5 @@
 import functools
+import math
 
 import jax
 import jax.numpy as jnp
@@ -10,6 +11,8 @@
 
 LANES = 128
 AXES = ("tm", "chan")
+WIDE = 2
+LATE = 4
 NT = (((1,), (1,)), ((), ()))
 NN = (((1,), (0,)), ((), ()))
 
@@ -90,79 +93,197 @@
     return high.reshape(rows_all, frame), low.reshape(rows_all, frame)
 
 
-def dft_kernel(owners, per, outer_ref, first_ref, second_ref, high_ref, low_ref, out_ref, th_ref, tl_ref):
-    many = max(1, 16 // per)
-    frame = high_ref.shape[1]
+def fill_table(owners, per, outer_ref, first_ref, second_ref, high_ref, low_ref):
+    many = 16 // math.gcd(per, 16)
+
+    def rows(step, carry):
+        parts = []
+        for extra in range(many):
+            owner = step * many + extra
+            cosine = outer_ref[0, pl.ds(owner, 1), :]
+            sine = outer_ref[1, pl.ds(owner, 1), :]
+            parts.append(first_ref[...] * cosine + second_ref[...] * sine)
+        value = parts[0] if many == 1 else jnp.concatenate(parts, axis=0)
+        high, low = halves(value)
+        at = pl.ds(pl.multiple_of(step * many * per, many * per), many * per)
+        high_ref[at, :] = high
+        low_ref[at, :] = low
+        return carry
+
+    lax.fori_loop(0, owners // many, rows, 0)
+
+
+def transform(owners, per, table_high, table_low, high, low, out_ref):
+    dot = functools.partial(lax.dot_general, dimension_numbers=NT, preferred_element_type=jnp.float32)
+    total = dot(table_high[...], high) + dot(table_high[...], low) + dot(table_low[...], high)
+    for block in range(WIDE):
+        part = total[:, block * LANES : (block + 1) * LANES]
+        out_ref[:, block * per : (block + 1) * per, :] = part.reshape(owners, per, LANES)
+
+
+def dft_kernel(owners, per, outer_ref, first_ref, second_ref, high_ref, low_ref, *rest):
+    out_ref, th_ref, tl_ref = rest[-3:]
 
     @pl.when(pl.program_id(0) == 0)
     def _():
-        def rows(step, carry):
-            parts = []
-            for extra in range(many):
-                owner = step * many + extra
-                cosine = outer_ref[0, pl.ds(owner, 1), :]
-                sine = outer_ref[1, pl.ds(owner, 1), :]
-                parts.append(first_ref[...] * cosine + second_ref[...] * sine)
-            value = parts[0] if many == 1 else jnp.concatenate(parts, axis=0)
-            high, low = halves(value)
-            at = pl.ds(pl.multiple_of(step * many * per, many * per), many * per)
-            th_ref[at, :] = high
-            tl_ref[at, :] = low
-            return carry
-
-        lax.fori_loop(0, owners // many, rows, 0)
-
-    dot = functools.partial(lax.dot_general, dimension_numbers=NT, preferred_element_type=jnp.float32)
-    total = dot(th_ref[...], high_ref[...])
-    total = total + dot(th_ref[...], low_ref[...])
-    total = total + dot(tl_ref[...], high_ref[...])
-    for block in range(out_ref.shape[1]):
-        part = total[:, block * LANES : (block + 1) * LANES]
-        out_ref[:, block] = part.reshape(owners, per, LANES)
-
-
-def dft_chunk(outer, first, second, high, low, owners, blocks):
+        fill_table(owners, per, outer_ref, first_ref, second_ref, th_ref, tl_ref)
+
+    transform(owners, per, th_ref, tl_ref, high_ref[...], low_ref[...], out_ref)
+
+
+def dft_chunk(outer, first, second, high, low, blocks, held, base, total_rows, token=None):
     per, frame = first.shape
-    wide = 2
-    rows = wide * LANES
+    owners = outer.shape[1]
+    rows = WIDE * LANES
+    skip = base // (WIDE * per)
     const = lambda b: (0, 0)
+    operands = [outer, first, second, high, low]
+    in_specs = [
+        pl.BlockSpec((2, owners, frame), lambda b: (0, 0, 0)),
+        pl.BlockSpec((per, frame), const),
+        pl.BlockSpec((per, frame), const),
+        pl.BlockSpec((rows, frame), lambda b: (b, 0)),
+        pl.BlockSpec((rows, frame), lambda b: (b, 0)),
+    ]
+    aliases = {}
+    if held is not None:
+        operands.append(held)
+        in_specs.append(pl.BlockSpec(memory_space=pl.ANY))
+        aliases = {5: 0}
+    if token is not None:
+        operands.append(token)
+        in_specs.append(pl.BlockSpec(memory_space=pl.ANY))
     return pl.pallas_call(
         functools.partial(dft_kernel, owners, per),
-        grid=(blocks // wide,),
-        in_specs=[
-            pl.BlockSpec((2, owners, frame), lambda b: (0, 0, 0)),
-            pl.BlockSpec((per, frame), const),
-            pl.BlockSpec((per, frame), const),
-            pl.BlockSpec((rows, frame), lambda b: (b, 0)),
-            pl.BlockSpec((rows, frame), lambda b: (b, 0)),
-        ],
-        out_specs=pl.BlockSpec((owners, wide, per, LANES), lambda b: (0, b, 0, 0)),
-        out_shape=jax.ShapeDtypeStruct((owners, blocks, per, LANES), jnp.float32),
+        grid=(blocks // WIDE,),
+        in_specs=in_specs,
+        out_specs=pl.BlockSpec((owners, WIDE * per, LANES), lambda b: (0, skip + b, 0)),
+        out_shape=jax.ShapeDtypeStruct((owners, total_rows, LANES), jnp.float32),
+        input_output_aliases=aliases,
         scratch_shapes=[
             pltpu.VMEM((owners * per, frame), jnp.bfloat16),
             pltpu.VMEM((owners * per, frame), jnp.bfloat16),
         ],
-        compiler_params=params(40),
+        compiler_params=params(48),
         cost_estimate=pl.CostEstimate(
             flops=6 * owners * per * frame * blocks * LANES,
             bytes_accessed=4 * blocks * LANES * frame + 4 * owners * blocks * per * LANES,
             transcendentals=0,
         ),
         name="dft_chunk",
-    )(outer, first, second, high, low)
-
-
-def correlate_kernel(sizes, scale, got_ref, *rest):
+    )(*operands)
+
+
+def first_kernel(owners, per, taps, groups, *refs):
+    now, before = refs[:groups], refs[groups : 2 * groups]
+    fir_ref, outer_ref, first_ref, second_ref, out_ref = refs[2 * groups : 2 * groups + 5]
+    th_ref, tl_ref, past_ref, high_ref, low_ref = refs[2 * groups + 5 :]
+    inputs = now[0].shape[0]
+    frame = fir_ref.shape[1]
+    edge = taps - 1
+
+    @pl.when(pl.program_id(0) == 0)
+    def _():
+        fill_table(owners, per, outer_ref, first_ref, second_ref, th_ref, tl_ref)
+        for group in range(groups):
+            past_ref[group] = before[group][:, (LATE - edge) * frame :]
+
+    rows = 16
+
+    def step(index, carry):
+        at = pl.ds(pl.multiple_of(index * rows, rows), rows)
+        for group in range(groups):
+
+            def sample(spec):
+                if spec < 0:
+                    return past_ref[group, at, (spec + edge) * frame : (spec + edge + 1) * frame]
+                return now[group][at, spec * frame : (spec + 1) * frame]
+
+            for spec in range(WIDE):
+                total = sample(spec) * fir_ref[0:1, :]
+                for tap in range(1, taps):
+                    total = total + sample(spec - tap) * fir_ref[tap : tap + 1, :]
+                high, low = halves(total)
+                place = pl.ds(pl.multiple_of(spec * LANES + group * inputs + index * rows, rows), rows)
+                high_ref[place, :] = high
+                low_ref[place, :] = low
+            kept = [sample(WIDE - edge + k) for k in range(edge)]
+            for k in range(edge):
+                past_ref[group, at, k * frame : (k + 1) * frame] = kept[k]
+        return carry
+
+    lax.fori_loop(0, inputs // rows, step, 0)
+    transform(owners, per, th_ref, tl_ref, high_ref[...], low_ref[...], out_ref)
+
+
+def first_chunk(outer, first, second, voltages, fir_taps, blocks, groups):
+    per, frame = first.shape
+    owners = outer.shape[1]
+    inputs, samples = voltages.shape
+    taps = fir_taps.shape[0]
+    kept = blocks - LATE
+    const = lambda b: (0, 0)
+
+    def now_map(group):
+        return lambda b: (0, (group * blocks + LATE) // WIDE + b)
+
+    def before_map(group):
+        return lambda b: (0, group * blocks // LATE)
+
+    return pl.pallas_call(
+        functools.partial(first_kernel, owners, per, taps, groups),
+        grid=(kept // WIDE,),
+        in_specs=[pl.BlockSpec((inputs, WIDE * frame), now_map(g)) for g in range(groups)]
+        + [pl.BlockSpec((inputs, LATE * frame), before_map(g)) for g in range(groups)]
+        + [
+            pl.BlockSpec((taps, frame), const),
+            pl.BlockSpec((2, owners, frame), lambda b: (0, 0, 0)),
+            pl.BlockSpec((per, frame), const),
+            pl.BlockSpec((per, frame), const),
+        ],
+        out_specs=pl.BlockSpec((owners, WIDE * per, LANES), lambda b: (0, b, 0)),
+        out_shape=jax.ShapeDtypeStruct((owners, kept * per, LANES), jnp.float32),
+        scratch_shapes=[
+            pltpu.VMEM((owners * per, frame), jnp.bfloat16),
+            pltpu.VMEM((owners * per, frame), jnp.bfloat16),
+            pltpu.VMEM((groups, inputs, (taps - 1) * frame), jnp.float32),
+            pltpu.VMEM((WIDE * LANES, frame), jnp.bfloat16),
+            pltpu.VMEM((WIDE * LANES, frame), jnp.bfloat16),
+        ],
+        compiler_params=params(48),
+        cost_estimate=pl.CostEstimate(
+            flops=6 * owners * per * frame * kept * LANES,
+            bytes_accessed=4 * inputs * samples,
+            transcendentals=0,
+        ),
+        name="first_chunk",
+    )(*([voltages] * (2 * groups)), fir_taps, outer, first, second)
+
+
+def correlate_kernel(sizes, scale, places, *refs):
     tm_count, chan_count, blocks, per, inputs = sizes
-    out_ref = rest[-1]
+    out_ref, token_ref, got_ref, sems = refs[-4:]
     channel = pl.program_id(0)
     groups = LANES // inputs
     channels = per // 2
+
+    @pl.when(channel == 0)
+    def _():
+        copies = []
+        for index, (base, rows, into) in enumerate(places):
+            source = refs[index].at[:, pl.ds(base, rows), :]
+            target = got_ref.at[:, pl.ds(into, rows), :]
+            copies.append(pltpu.make_async_copy(source, target, sems.at[index]))
+            copies[-1].start()
+        for copy in copies:
+            copy.wait()
+        token_ref[...] = jnp.zeros_like(token_ref)
+
     lane_group = lax.broadcasted_iota(jnp.int32, (blocks, LANES), 1) // inputs
 
     def piece(time, chan, part):
-        start = (time * chan_count + chan) * blocks * per + part * channels + channel
-        return got_ref[pl.ds(start, blocks, stride=per), :]
+        rows = pl.ds(part * channels + channel, blocks, stride=per)
+        return got_ref[time * chan_count + chan, rows, :]
 
     def tile(time, part, column):
         held = [piece(time, column * groups + place, part) for place in range(groups)]
@@ -198,37 +319,51 @@
         out_ref[0, which] = total * scale
 
 
-def correlate_chunk(got, held, start, owned, sizes, spectra):
+def correlate_chunk(pieces, held, start, owned, sizes, spectra):
     tm_count, chan_count, blocks, per, inputs = sizes
     channels = per // 2
     everyone = chan_count * inputs
-    rows = got.shape[0] * got.shape[1] * got.shape[2]
-    first = start // channels
-    operands = [got.reshape(rows, LANES)]
-    in_specs = [pl.BlockSpec((rows, LANES), lambda c: (0, 0))]
+    owners = tm_count * chan_count
+    operands = [piece[0] for piece in pieces]
+    places = [piece[1:] for piece in pieces]
     aliases = {}
     if held is not None:
+        aliases = {len(operands): 0}
         operands.append(held)
-        in_specs.append(pl.BlockSpec(memory_space=pl.ANY))
-        aliases = {1: 0}
     return pl.pallas_call(
-        functools.partial(correlate_kernel, sizes, 1.0 / spectra),
+        functools.partial(correlate_kernel, sizes, 1.0 / spectra, places),
         grid=(channels,),
-        in_specs=in_specs,
-        out_specs=pl.BlockSpec((1, 2, everyone, everyone), lambda c: (start + c, 0, 0, 0)),
-        out_shape=jax.ShapeDtypeStruct((owned, 2, everyone, everyone), jnp.float32),
+        in_specs=[pl.BlockSpec(memory_space=pl.ANY)] * len(operands),
+        out_specs=[
+            pl.BlockSpec((1, 2, everyone, everyone), lambda c: (start + c, 0, 0, 0)),
+            pl.BlockSpec((8, LANES), lambda c: (0, 0)),
+        ],
+        out_shape=[
+            jax.ShapeDtypeStruct((owned, 2, everyone, everyone), jnp.float32),
+            jax.ShapeDtypeStruct((8, LANES), jnp.float32),
+        ],
         input_output_aliases=aliases,
+        scratch_shapes=[
+            pltpu.VMEM((owners, blocks * per, LANES), jnp.float32),
+            pltpu.SemaphoreType.DMA((len(pieces),)),
+        ],
         compiler_params=params(40),
         cost_estimate=pl.CostEstimate(
             flops=6 * channels * 2 * everyone * everyone * 2 * spectra,
-            bytes_accessed=channels * 8 * everyone * everyone + 4 * rows * LANES,
+            bytes_accessed=channels * 8 * everyone * everyone + 4 * owners * blocks * per * LANES,
             transcendentals=0,
         ),
         name="correlate_chunk",
     )(*operands)
 
 
-def phases(frame, owners, owned, chunk):
+def chunk_sizes(owned):
+    if owned % 32 == 0:
+        return [owned // 8, owned // 4, owned // 2, owned // 8]
+    return [4] * (owned // 4)
+
+
+def phases(frame, owners, owned, sizes):
     samples = np.arange(frame)
     outer = 2.0 * np.pi * ((np.arange(owners)[:, None] * owned * samples) % frame) / frame
     inner = 2.0 * np.pi * ((np.arange(owned)[:, None] * samples) % frame) / frame
@@ -236,11 +371,13 @@
     cosine, sine = np.cos(inner) * scale, np.sin(inner) * scale
     outer = np.stack([np.cos(outer), np.sin(outer)]).astype(np.float32)
     tables = []
-    for start in range(0, owned, chunk):
-        here = slice(start, start + chunk)
+    start = 0
+    for size in sizes:
+        here = slice(start, start + size)
         first = np.concatenate([cosine[here], -sine[here]]).astype(np.float32)
         second = np.concatenate([-sine[here], -cosine[here]]).astype(np.float32)
         tables.append((start, first, second))
+        start += size
     return outer, tables
 
 
@@ -253,18 +390,53 @@
     owned = frame // 2 // owners
     groups = LANES // inputs
     blocks = spec_dev // groups
-    chunk = max(4, owned // 4)
+    chunks = chunk_sizes(owned)
+    outer, tables = phases(frame, owners, owned, chunks)
+    split = blocks >= 2 * LATE and len(chunks) > 1
+
+    def exchange(value):
+        return lax.all_to_all(value, AXES, split_axis=0, concat_axis=0, tiled=True)
+
     halo = passed_along(voltages[:, samples - (taps - 1) * frame :], "tm", 1)
+    if split:
+        ahead = first_chunk(outer, *tables[0][1:], voltages, fir_taps, blocks, groups)
+        ahead, halo = lax.optimization_barrier((ahead, halo))
     high, low = filtered_parts(voltages, halo, fir_taps, blocks, groups)
-    outer, tables = phases(frame, owners, owned, chunk)
-    sizes = (tm_count, chan_count, blocks, 2 * chunk, inputs)
-    moved = []
-    for start, first, second in tables:
-        made = dft_chunk(outer, first, second, high, low, owners, blocks)
-        moved.append((start, lax.all_to_all(made, AXES, split_axis=0, concat_axis=0, tiled=True)))
-    out = None
-    for start, got in moved:
-        out = correlate_chunk(got, out, start, owned, sizes, tm_count * spec_dev)
+
+    pieces = [[] for _ in chunks]
+    out, token, correlated = None, None, 0
+
+    def correlate(index):
+        nonlocal out, token
+        sizes = (tm_count, chan_count, blocks, 2 * chunks[index], inputs)
+        out, token = correlate_chunk(
+            pieces[index], out, tables[index][0], owned, sizes, tm_count * spec_dev
+        )
+
+    for index, (start, first, second) in enumerate(tables):
+        per = 2 * chunks[index]
+        rows = blocks * per
+        if index == 0 and split:
+            got = exchange(ahead)
+            pieces[0].append((got, 0, (blocks - LATE) * per, LATE * per))
+            continue
+        while correlated <= index - 2 and (index > 2 or not split):
+            correlate(correlated)
+            correlated += 1
+        if index == 1 and split:
+            more = LATE * 2 * chunks[0]
+            made = dft_chunk(outer, *tables[0][1:], high, low, LATE, None, rows, rows + more)
+            made = dft_chunk(outer, first, second, high, low, blocks, made, 0, rows + more)
+        else:
+            more = 0
+            made = dft_chunk(outer, first, second, high, low, blocks, None, 0, rows, token)
+        got = exchange(made)
+        if more:
+            pieces[0].append((got, rows, more, 0))
+        pieces[index].append((got, 0, rows, 0))
+    while correlated < len(chunks):
+        correlate(correlated)
+        correlated += 1
     return out
 
 

time: 476 us -> 439 us (0.922)
  waiting for transfers between devices: 277 us -> 250 us
  Pallas kernels: 138 us -> 154 us
  starting transfers between devices: 37.2 us -> 21.9 us
  local copies, waits for them, and re-layouts: 23.6 us -> 11.9 us
    all_to_all x4, waiting for transfers between devices: 274 us -> 250 us  [exchange(): return lax.all_to_all(value, AXES, split_axis=0, concat_axis=0, tiled=True)]
    pallas_call x4 -> x5, Pallas kernels: 55.6 us -> 74.7 us  [the longest x4 57.6 us: correlate_chunk(): pl.pallas_call(functools.partial(correlate_kernel, sizes, 1.0 / spectra,...]
    all_to_all x4, starting transfers between devices: 34.7 us -> 19.4 us  [exchange(): return lax.all_to_all(value, AXES, split_axis=0, concat_axis=0, tiled=True)]
    unnamed x36 -> x34, local copies, waits for them, and re-layouts: 22 us -> 10.4 us
  transfers between devices with their start and end apart: 5 -> 5, of which waited for: 5 -> 3; matrix products, arithmetic and copies ran while one was open for 0% -> 0% of each run, Pallas kernels for 20% -> 34%
where the time goes in v2:
time: 439 us; the launch traced here: 438 us
  waiting for transfers between devices  250 us (57%)
  Pallas kernels  154 us (35%)
  starting transfers between devices  21.9 us (5%)
  local copies, waits for them, and re-layouts  11.9 us (3%)
    all_to_all x4, waiting for transfers between devices, exchange(): return lax.all_to_all(value, AXES, split_axis=0, concat_axis=0, tiled=True)  250 us
    pallas_call x4, Pallas kernels, dft_chunk(): pl.pallas_call(functools.partial(dft_kernel, owners, per), grid=(blocks /...  66.9 us
    pallas_call x4, Pallas kernels, correlate_chunk(): pl.pallas_call(functools.partial(correlate_kernel, sizes, 1.0 / spectra,...  57.6 us
    all_to_all x4, starting transfers between devices, exchange(): return lax.all_to_all(value, AXES, split_axis=0, concat_axis=0, tiled=True)  19.4 us
    pallas_call x1, Pallas kernels, first_chunk(): pl.pallas_call(functools.partial(first_kernel, owners, per, taps, groups)...  17.1 us
    pallas_call x1, Pallas kernels, filtered_parts(): pl.pallas_call(functools.partial(filter_kernel, blocks, groups, taps), gr...  12.8 us
    unnamed x34, local copies, waits for them, and re-layouts  10.4 us
  transfers between devices with their start and end apart: 5, of which 3 were waited for; matrix products, arithmetic and copies ran while one was open for 0% of the time, Pallas kernels for 34%

profile of v2, /device:TPU:0, one launch (start us, length us, event | category | flops | bytes accessed | tf_op | source)
XLA Modules:
  0.0 438.0 jit_solution(8351008729404106355)
XLA Ops:
  0.0 1.5 slice.3
  1.5 2.5 collective-permute-start
  4.0 0.0 copy-start.2
  4.0 1.0 copy-done.2
  5.0 0.0 copy-start.5
  5.0 0.8 copy-done.5
  5.9 0.8 copy-done.7
  6.7 0.8 copy-done.9
  7.5 17.1 %first_chunk.1 = f32[32,96,128]{2,1,0:T(8,128)} custom-call(f32[64,65536]{1,0:T(8,128)} %volt_ref.1, f32[64,65536]{1,0:T(8,128)} %volt_ref.1, f32[64,65536]{1,0:T(8,128)} %volt_ref.1, f32[64,65536]{1,0:T(8,128)} %volt_ref.1, f32[4,2048]{1,0:T(4,128)S(1)} %copy-done.9, f32[2,32,2048]{2,1,0:T(8,128)S(1)} %copy-done.2, f32[8,2048]{1,0:T(8,128)S(1)} %copy-done.5, ...), custom_call_target="tpu_custom_call" | custom-call | flops 4831838208 | bytes 16777216 | tf_op jit(solution)/shard_map/first_chunk/pallas_call | solution.py:233
  24.6 0.0 collective-permute-done.halo_ref
  24.6 7.1 %all-to-all-start.1 = ((f32[32,96,128]{2,1,0:T(8,128)}), f32[32,96,128]{2,1,0:T(8,128)}, u32[]{:S(2)}, u32[]{:S(2)}) async-start(f32[32,96,128]{2,1,0:T(8,128)} %first_chunk.1), calls=%async_computation.1 | async-start | bytes 3145728 | tf_op jit(solution)/shard_map/all_to_all | solution.py:398
  31.7 0.0 copy-done.10
  31.8 0.0 copy-start.3
  31.8 0.0 copy-start.6
  31.8 0.0 copy-start.8
  31.8 12.8 %polyphase_filter.1 = (bf16[16,2,64,2048]{3,2,1,0:T(8,128)(2,1)S(1)}, bf16[16,2,64,2048]{3,2,1,0:T(8,128)(2,1)}) custom-call(f32[64,65536]{1,0:T(8,128)} %volt_ref.1, f32[64,6144]{1,0:T(8,128)S(1)} %collective-permute-done.halo_ref, f32[4,2048]{1,0:T(4,128)S(1)} %copy-done.10), custom_call_target="tpu_custom_call" | custom-call | flops 33554432 | bytes 33554432 | tf_op jit(solution)/shard_map/polyphase_filter/pallas_call | solution.py:76
  44.6 3.3 copy-done.1
  47.9 0.0 copy-done.3
  47.9 0.0 copy-done.6
  47.9 0.0 copy-done.8
  47.9 0.0 copy-start.14
  47.9 4.4 %dft_chunk.4.rest_0_ = f32[32,288,128]{2,1,0:T(8,128)S(1)} custom-call(f32[2,32,2048]{2,1,0:T(8,128)S(1)} %copy-done.3, f32[8,2048]{1,0:T(8,128)S(1)} %copy-done.6, f32[8,2048]{1,0:T(8,128)S(1)} %copy-done.8, bf16[2048,2048]{1,0:T(8,128)(2,1)} %bitcast.2, bf16[2048,2048]{1,0:T(8,128)(2,1)} %bitcast.6), custom_call_target="tpu_custom_call" | custom-call | flops 1610612736 | bytes 4718592 | tf_op jit(solution)/shard_map/dft_chunk/pallas_call | solution.py:156
  52.4 0.0 copy-done.13
  52.4 0.0 copy-done.14
  52.4 17.7 %dft_chunk.5 = f32[32,288,128]{2,1,0:T(8,128)S(1)} custom-call(f32[2,32,2048]{2,1,0:T(8,128)S(1)} %copy-done.3, f32[16,2048]{1,0:T(8,128)S(1)} %copy-done.13, f32[16,2048]{1,0:T(8,128)S(1)} %copy-done.14, bf16[2048,2048]{1,0:T(8,128)(2,1)} %bitcast.3, bf16[2048,2048]{1,0:T(8,128)(2,1)} %bitcast.7, ...), custom_call_target="tpu_custom_call", output_to_operand_aliasing={{}: (5, {})} | custom-call | flops 12884901888 | bytes 20971520 | tf_op jit(solution)/shard_map/dft_chunk/pallas_call | solution.py:156
  70.0 0.0 copy-start
  70.1 2.2 copy-done
  72.2 0.0 all-to-all-done.1.refs_0_
  72.2 5.9 %all-to-all-start = ((f32[32,288,128]{2,1,0:T(8,128)}), f32[32,288,128]{2,1,0:T(8,128)}, u32[]{:S(2)}, u32[]{:S(2)}) async-start(f32[32,288,128]{2,1,0:T(8,128)} %copy-done), calls=%async_computation | async-start | bytes 9437184 | tf_op jit(solution)/shard_map/all_to_all | solution.py:398
  78.1 0.0 copy-done.11
  78.2 0.0 copy-done.12
  78.2 32.5 %dft_chunk.7 = f32[32,512,128]{2,1,0:T(8,128)} custom-call(f32[2,32,2048]{2,1,0:T(8,128)S(1)} %copy-done.3, f32[32,2048]{1,0:T(8,128)S(1)} %copy-done.11, f32[32,2048]{1,0:T(8,128)S(1)} %copy-done.12, bf16[2048,2048]{1,0:T(8,128)(2,1)} %bitcast.4, bf16[2048,2048]{1,0:T(8,128)(2,1)} %bitcast.8), custom_call_target="tpu_custom_call" | custom-call | flops 25769803776 | bytes 25165824 | tf_op jit(solution)/shard_map/dft_chunk/pallas_call | solution.py:156
  110.6 75.0 %all-to-all-done.refs_1_.refs_0_ = f32[32,288,128]{2,1,0:T(8,128)} async-done(((f32[32,288,128]{2,1,0:T(8,128)}), f32[32,288,128]{2,1,0:T(8,128)}, u32[]{:S(2)}, u32[]{:S(2)}) %all-to-all-start) | async-done | bytes 4718624 | tf_op jit(solution)/shard_map/all_to_all | solution.py:398
  185.7 3.7 all-to-all-start.3
  189.4 7.7 %correlate_chunk.4 = (f32[32,2,512,512]{3,2,1,0:T(8,128)}, f32[8,128]{1,0:T(8,128)}) custom-call(f32[32,96,128]{2,1,0:T(8,128)} %all-to-all-done.1.refs_0_, f32[32,288,128]{2,1,0:T(8,128)} %all-to-all-done.refs_1_.refs_0_), custom_call_target="tpu_custom_call" | custom-call | flops 3221225472 | bytes 10485760 | tf_op jit(solution)/shard_map/correlate_chunk/pallas_call | solution.py:333
  197.1 0.0 copy-start.15
  197.1 0.0 copy-start.16
  197.1 13.9 %correlate_chunk.5 = (f32[32,2,512,512]{3,2,1,0:T(8,128)}, f32[8,128]{1,0:T(8,128)S(1)}) custom-call(f32[32,288,128]{2,1,0:T(8,128)} %all-to-all-done.refs_1_.refs_0_, f32[32,2,512,512]{3,2,1,0:T(8,128)} %get-tuple-element.18.refs_1_), custom_call_target="tpu_custom_call", output_to_operand_aliasing={{0}: (1, {})} | custom-call | flops 6442450944 | bytes 20971520 | tf_op jit(solution)/shard_map/correlate_chunk/pallas_call | solution.py:333
  211.0 0.0 copy-done.15
  211.0 0.0 copy-done.16
  211.1 12.4 %dft_chunk.6 = f32[32,128,128]{2,1,0:T(8,128)S(1)} custom-call(f32[2,32,2048]{2,1,0:T(8,128)S(1)} %copy-done.3, f32[8,2048]{1,0:T(8,128)S(1)} %copy-done.15, f32[8,2048]{1,0:T(8,128)S(1)} %copy-done.16, bf16[2048,2048]{1,0:T(8,128)(2,1)} %bitcast.5, bf16[2048,2048]{1,0:T(8,128)(2,1)} %bitcast.9, f32[8,128]{1,0:T(8,128)S(1)} %get-tuple-element.19.rest_0_), custom_call_target="tpu_custom_call" | custom-call | flops 6442450944 | bytes 18874368 | tf_op jit(solution)/shard_map/dft_chunk/pallas_call | solution.py:156
  223.4 0.0 copy-start.4
  223.4 1.4 copy-done.4
  224.8 154.0 %all-to-all-done.3.refs_0_ = f32[32,512,128]{2,1,0:T(8,128)} async-done(((f32[32,512,128]{2,1,0:T(8,128)}), f32[32,512,128]{2,1,0:T(8,128)}, u32[]{:S(2)}, u32[]{:S(2)}) %all-to-all-start.3) | async-done | bytes 8388640 | tf_op jit(solution)/shard_map/all_to_all | solution.py:398
  378.8 2.7 all-to-all-start.2
  381.6 29.6 %correlate_chunk.6 = (f32[32,2,512,512]{3,2,1,0:T(8,128)}, f32[8,128]{1,0:T(8,128)}) custom-call(f32[32,512,128]{2,1,0:T(8,128)} %all-to-all-done.3.refs_0_, f32[32,2,512,512]{3,2,1,0:T(8,128)} %get-tuple-element.20.refs_1_), custom_call_target="tpu_custom_call", output_to_operand_aliasing={{0}: (1, {})} | custom-call | flops 12884901888 | bytes 41943040 | tf_op jit(solution)/shard_map/correlate_chunk/pallas_call | solution.py:333
  411.2 20.5 %all-to-all-done.2.refs_0_ = f32[32,128,128]{2,1,0:T(8,128)S(1)} async-done(((f32[32,128,128]{2,1,0:T(8,128)}), f32[32,128,128]{2,1,0:T(8,128)S(1)}, u32[]{:S(2)}, u32[]{:S(2)}) %all-to-all-start.2) | async-done | bytes 2097184 | tf_op jit(solution)/shard_map/all_to_all | solution.py:398
  431.6 6.3 %correlate_chunk.7 = (f32[32,2,512,512]{3,2,1,0:T(8,128)}, f32[8,128]{1,0:T(8,128)}) custom-call(f32[32,128,128]{2,1,0:T(8,128)S(1)} %all-to-all-done.2.refs_0_, f32[32,2,512,512]{3,2,1,0:T(8,128)} %get-tuple-element.21.refs_1_), custom_call_target="tpu_custom_call", output_to_operand_aliasing={{0}: (1, {})} | custom-call | flops 3221225472 | bytes 10485760 | tf_op jit(solution)/shard_map/correlate_chunk/pallas_call | solution.py:333
  (7 shorter events, 0.0 us)
Async XLA Ops:
  1.5 23.1 %collective-permute-start = (f32[64,6144]{1,0:T(8,128)S(1)}, f32[64,6144]{1,0:T(8,128)S(1)}, u32[]{:S(2)}, u32[]{:S(2)}) collective-permute-start(f32[64,6144]{1,0:T(8,128)S(1)} %slice.3), channel_id=1, source_target_pairs={{0,8},{8,16},{16,24},{1,9},{9,17},{17,25},{2,10},{10,18},{18,26},{... | collective-permute-start | bytes 4718600 | tf_op jit(solution)/shard_map/ppermute | solution.py:33
  4.0 1.0 copy-start.2
  5.0 0.8 copy-start.5
  5.9 0.8 copy-start.7
  6.7 0.8 copy-start.9
  7.5 24.3 %copy-start.10 = (f32[4,2048]{1,0:T(4,128)S(1)}, f32[4,2048]{1,0:T(4,128)}, u32[]{:S(2)}) copy-start(f32[4,2048]{1,0:T(4,128)} %fir_ref.1) | copy-start | bytes 98308
  24.6 47.7 %all-to-all-start.1 = ((f32[32,96,128]{2,1,0:T(8,128)}), f32[32,96,128]{2,1,0:T(8,128)}, u32[]{:S(2)}, u32[]{:S(2)}) async-start(f32[32,96,128]{2,1,0:T(8,128)} %first_chunk.1), calls=%async_computation.1 | async-start | bytes 3145728 | tf_op jit(solution)/shard_map/all_to_all | solution.py:398
  31.8 16.2 %copy-start.3 = (f32[2,32,2048]{2,1,0:T(8,128)S(1)}, f32[2,32,2048]{2,1,0:T(8,128)}, u32[]{:S(2)}) copy-start(f32[2,32,2048]{2,1,0:T(8,128)} %constant.18.clone.refs_5_.outer_ref) | copy-start | bytes 1572868
  31.8 16.1 %copy-start.6 = (f32[8,2048]{1,0:T(8,128)S(1)}, f32[8,2048]{1,0:T(8,128)}, u32[]{:S(2)}) copy-start(f32[8,2048]{1,0:T(8,128)} %constant.19.clone.refs_6_.first_ref) | copy-start | bytes 196612
  31.8 16.1 %copy-start.8 = (f32[8,2048]{1,0:T(8,128)S(1)}, f32[8,2048]{1,0:T(8,128)}, u32[]{:S(2)}) copy-start(f32[8,2048]{1,0:T(8,128)} %constant.20.clone.refs_7_.second_ref) | copy-start | bytes 196612
  44.6 3.3 copy-start.1
  47.9 4.4 %copy-start.13 = (f32[16,2048]{1,0:T(8,128)S(1)}, f32[16,2048]{1,0:T(8,128)}, u32[]{:S(2)}) copy-start(f32[16,2048]{1,0:T(8,128)} %constant.21.clone.first_ref) | copy-start | bytes 393220
  47.9 4.4 %copy-start.14 = (f32[16,2048]{1,0:T(8,128)S(1)}, f32[16,2048]{1,0:T(8,128)}, u32[]{:S(2)}) copy-start(f32[16,2048]{1,0:T(8,128)} %constant.22.clone.second_ref) | copy-start | bytes 393220
  70.0 2.2 copy-start
  72.2 5.9 %copy-start.11 = (f32[32,2048]{1,0:T(8,128)S(1)}, f32[32,2048]{1,0:T(8,128)}, u32[]{:S(2)}) copy-start(f32[32,2048]{1,0:T(8,128)} %constant.23.clone.first_ref) | copy-start | bytes 786436
  72.2 5.9 %copy-start.12 = (f32[32,2048]{1,0:T(8,128)S(1)}, f32[32,2048]{1,0:T(8,128)}, u32[]{:S(2)}) copy-start(f32[32,2048]{1,0:T(8,128)} %constant.24.clone.second_ref) | copy-start | bytes 786436
  72.2 113.4 %all-to-all-start = ((f32[32,288,128]{2,1,0:T(8,128)}), f32[32,288,128]{2,1,0:T(8,128)}, u32[]{:S(2)}, u32[]{:S(2)}) async-start(f32[32,288,128]{2,1,0:T(8,128)} %copy-done), calls=%async_computation | async-start | bytes 9437184 | tf_op jit(solution)/shard_map/all_to_all | solution.py:398
  185.7 193.2 %all-to-all-start.3 = ((f32[32,512,128]{2,1,0:T(8,128)}), f32[32,512,128]{2,1,0:T(8,128)}, u32[]{:S(2)}, u32[]{:S(2)}) async-start(f32[32,512,128]{2,1,0:T(8,128)} %dft_chunk.7), calls=%async_computation.3 | async-start | bytes 16777216 | tf_op jit(solution)/shard_map/all_to_all | solution.py:398
  197.1 14.0 %copy-start.15 = (f32[8,2048]{1,0:T(8,128)S(1)}, f32[8,2048]{1,0:T(8,128)}, u32[]{:S(2)}) copy-start(f32[8,2048]{1,0:T(8,128)} %constant.25.clone.first_ref) | copy-start | bytes 196612
  197.1 14.0 %copy-start.16 = (f32[8,2048]{1,0:T(8,128)S(1)}, f32[8,2048]{1,0:T(8,128)}, u32[]{:S(2)}) copy-start(f32[8,2048]{1,0:T(8,128)} %constant.26.clone.second_ref) | copy-start | bytes 196612
  223.4 1.4 copy-start.4
  378.8 52.8 %all-to-all-start.2 = ((f32[32,128,128]{2,1,0:T(8,128)}), f32[32,128,128]{2,1,0:T(8,128)S(1)}, u32[]{:S(2)}, u32[]{:S(2)}) async-start(f32[32,128,128]{2,1,0:T(8,128)} %copy-done.4), calls=%async_computation.2 | async-start | bytes 4194304 | tf_op jit(solution)/shard_map/all_to_all | solution.py:398

commit v3 on v2

v3 whole, which is shorter than its diff:
```python
import functools
import math

import jax
import jax.numpy as jnp
import numpy as np
from jax import lax
from jax.experimental import pallas as pl
from jax.experimental.pallas import tpu as pltpu
from jax.sharding import PartitionSpec as P

LANES = 128
AXES = ("tm", "chan")
PAIR = 2
WIDE = 2
LATE = 6
NT = (((1,), (1,)), ((), ()))
NN = (((1,), (0,)), ((), ()))


def params(mib):
    return pltpu.CompilerParams(vmem_limit_bytes=mib << 20)


def halves(value):
    high = value.astype(jnp.bfloat16)
    low = (value - high.astype(jnp.float32)).astype(jnp.bfloat16)
    return high, low


def passed_along(value, axis, steps):
    count = lax.axis_size(axis)
    first, last = (max(0, -steps), min(count, count - steps))
    return lax.ppermute(value, axis, [(source, source + steps) for source in range(first, last)])


def weighted(frames, weights):
    total = frames[0] * weights[0]
    for frame, weight in zip(frames[1:], weights[1:]):
        total = total + frame * weight
    return total


def folded(left, right):
    return halves(left + right) + halves(left - right)


def filter_kernel(blocks, groups, taps, volt_ref, halo_ref, fir_ref, *out_refs):
    rows = volt_ref.shape[0]
    frame = fir_ref.shape[1]
    edge = taps - 1
    width = 2 * LANES

    def columns(column, carry):
        begins = [pl.multiple_of(column * width, width), pl.multiple_of(column * width + frame // 2, width)]
        here = pl.ds(begins[0], width)
        weights = [
            [jnp.broadcast_to(fir_ref[tap : tap + 1, pl.ds(begin, width)], (rows, width)) for tap in range(taps)]
            for begin in begins
        ]

        def step(spec, past):
            now = [volt_ref[:, pl.ds(pl.multiple_of(spec * frame + begin, width), width)] for begin in begins]
            sides = [weighted((now[k],) + past[k], weights[k]) for k in range(2)]
            block, group = lax.rem(spec, blocks), lax.div(spec, blocks)
            for ref, value in zip(out_refs, folded(*sides)):
                ref[block, group, :, here] = value
            return tuple((now[k],) + past[k][:-1] for k in range(2))

        past = tuple(
            tuple(
                halo_ref[:, pl.ds(pl.multiple_of((edge - 1 - k) * frame + begin, width), width)]
                for k in range(edge)
            )
            for begin in begins
        )
        lax.fori_loop(0, blocks * groups, step, past, unroll=4)
        return carry

    lax.fori_loop(0, frame // 2 // width, columns, 0)


def filtered_parts(voltages, halo, fir_taps, blocks, groups):
    inputs, samples = voltages.shape
    taps, frame = fir_taps.shape
    rows = 16
    shape = jax.ShapeDtypeStruct((blocks, groups, inputs, frame // 2), jnp.bfloat16)
    out_spec = pl.BlockSpec((blocks, groups, rows, frame // 2), lambda g: (0, 0, g, 0))
    made = pl.pallas_call(
        functools.partial(filter_kernel, blocks, groups, taps),
        grid=(inputs // rows,),
        in_specs=[
            pl.BlockSpec((rows, samples), lambda g: (g, 0)),
            pl.BlockSpec((rows, halo.shape[1]), lambda g: (g, 0)),
            pl.BlockSpec((taps, frame), lambda g: (0, 0)),
        ],
        out_specs=[out_spec] * 4,
        out_shape=[shape] * 4,
        compiler_params=params(48),
        cost_estimate=pl.CostEstimate(
            flops=8 * inputs * samples, bytes_accessed=8 * inputs * samples, transcendentals=0
        ),
        name="polyphase_filter",
    )(voltages, halo, fir_taps)
    made = [part.reshape(blocks * groups * inputs, frame // 2) for part in made]
    return made[:2], made[2:]


def fill_table(owners, per, outer_ref, first_ref, second_ref, high_ref, low_ref):
    many = 16 // math.gcd(per, 16)

    def rows(step, carry):
        parts = []
        for extra in range(many):
            owner = step * many + extra
            cosine = outer_ref[0, pl.ds(owner, 1), :]
            sine = outer_ref[1, pl.ds(owner, 1), :]
            parts.append(first_ref[...] * cosine + second_ref[...] * sine)
        value = parts[0] if many == 1 else jnp.concatenate(parts, axis=0)
        high, low = halves(value)
        at = pl.ds(pl.multiple_of(step * many * per, many * per), many * per)
        high_ref[at, :] = high
        low_ref[at, :] = low
        return carry

    lax.fori_loop(0, owners // many, rows, 0)


def transform(owners, per, table_high, table_low, high, low, out_ref):
    dot = functools.partial(lax.dot_general, dimension_numbers=NT, preferred_element_type=jnp.float32)
    total = dot(table_high[...], high) + dot(table_high[...], low) + dot(table_low[...], high)
    for block in range(WIDE):
        part = total[:, block * LANES : (block + 1) * LANES]
        out_ref[:, block * per : (block + 1) * per, :] = part.reshape(owners, per, LANES)


def dft_kernel(owners, per, outer_ref, first_ref, second_ref, high_ref, low_ref, *rest):
    out_ref, th_ref, tl_ref = rest[-3:]

    @pl.when(pl.program_id(0) == 0)
    def _():
        fill_table(owners, per, outer_ref, first_ref, second_ref, th_ref, tl_ref)

    transform(owners, per, th_ref, tl_ref, high_ref[...], low_ref[...], out_ref)


def dft_chunk(outer, first, second, high, low, blocks, held, base, total_rows, token=None):
    per, frame = first.shape
    owners = outer.shape[1]
    rows = WIDE * LANES
    assert base % (WIDE * per) == 0
    skip = base // (WIDE * per)
    const = lambda b: (0, 0)
    operands = [outer, first, second, high, low]
    in_specs = [
        pl.BlockSpec((2, owners, frame), lambda b: (0, 0, 0)),
        pl.BlockSpec((per, frame), const),
        pl.BlockSpec((per, frame), const),
        pl.BlockSpec((rows, frame), lambda b: (b, 0)),
        pl.BlockSpec((rows, frame), lambda b: (b, 0)),
    ]
    aliases = {}
    if held is not None:
        operands.append(held)
        in_specs.append(pl.BlockSpec(memory_space=pl.ANY))
        aliases = {5: 0}
    if token is not None:
        operands.append(token)
        in_specs.append(pl.BlockSpec(memory_space=pl.ANY))
    return pl.pallas_call(
        functools.partial(dft_kernel, owners, per),
        grid=(blocks // WIDE,),
        in_specs=in_specs,
        out_specs=pl.BlockSpec((owners, WIDE * per, LANES), lambda b: (0, skip + b, 0)),
        out_shape=jax.ShapeDtypeStruct((owners, total_rows, LANES), jnp.float32),
        input_output_aliases=aliases,
        scratch_shapes=[
            pltpu.VMEM((owners * per, frame), jnp.bfloat16),
            pltpu.VMEM((owners * per, frame), jnp.bfloat16),
        ],
        compiler_params=params(60),
        cost_estimate=pl.CostEstimate(
            flops=6 * owners * per * frame * blocks * LANES,
            bytes_accessed=4 * blocks * LANES * frame + 4 * owners * blocks * per * LANES,
            transcendentals=0,
        ),
        name="dft_chunk",
    )(*operands)


def first_kernel(owners, per, taps, groups, *refs):
    now = refs[:groups]
    fir_ref, outer_ref, first_ref, second_ref, out_ref = refs[groups : groups + 5]
    th_ref, tl_ref, past_ref, high_ref, low_ref = refs[groups + 5 :]
    inputs = now[0].shape[0]
    frame = fir_ref.shape[1]
    edge = taps - 1
    pair = pl.program_id(0)
    ahead = pl.cdiv(edge, WIDE)

    @pl.when(pair == 0)
    def _():
        fill_table(owners, per, outer_ref, first_ref, second_ref, th_ref, tl_ref)

    @pl.when(pair < ahead)
    def _():
        @pl.when(pair > 0)
        def _():
            for k in range(edge - WIDE):
                past_ref[k] = past_ref[k + WIDE]

        for group in range(groups):
            for k in range(WIDE):
                past_ref[edge - WIDE + k, group] = now[group][:, k * frame : (k + 1) * frame]

    @pl.when(pair >= ahead)
    def _():
        rows = 16
        width = 2 * LANES

        def columns(column, carry):
            begins = [
                pl.multiple_of(column * width, width),
                pl.multiple_of(column * width + frame // 2, width),
            ]
            weights = [
                [
                    jnp.broadcast_to(fir_ref[tap : tap + 1, pl.ds(begin, width)], (rows, width))
                    for tap in range(taps)
                ]
                for begin in begins
            ]
            for group in range(groups):
                for start in range(0, inputs, rows):
                    at = pl.ds(start, rows)
                    sums = [None] * WIDE
                    for begin, weight in zip(begins, weights):
                        here = pl.ds(begin, width)
                        frames = [past_ref[k, group, at, here] for k in range(edge)]
                        for spec in range(WIDE):
                            frames.append(
                                now[group][at, pl.ds(pl.multiple_of(spec * frame + begin, width), width)]
                            )
                        for spec in range(WIDE):
                            total = weighted([frames[edge + spec - tap] for tap in range(taps)], weight)
                            sums[spec] = total if sums[spec] is None else sums[spec] + total
                        for k in range(edge):
                            past_ref[k, group, at, here] = frames[WIDE + k]
                    for spec in range(WIDE):
                        high, low = halves(sums[spec])
                        place = pl.ds(spec * LANES + group * inputs + start, rows)
                        high_ref[place, pl.ds(begins[0], width)] = high
                        low_ref[place, pl.ds(begins[0], width)] = low
            return carry

        lax.fori_loop(0, frame // 2 // width, columns, 0)
        transform(owners, per, th_ref, tl_ref, high_ref[...], low_ref[...], out_ref)


def first_chunk(outer, first, second, voltages, fir_taps, blocks, groups):
    per, half = first.shape
    owners = outer.shape[1]
    inputs, samples = voltages.shape
    taps, frame = fir_taps.shape
    kept = blocks - LATE
    const = lambda b: (0, 0)

    ahead = pl.cdiv(taps - 1, WIDE)

    def now_map(group):
        return lambda b: (0, (group * blocks + LATE) // WIDE - ahead + b)

    return pl.pallas_call(
        functools.partial(first_kernel, owners, per, taps, groups),
        grid=(kept // WIDE + ahead,),
        in_specs=[pl.BlockSpec((inputs, WIDE * frame), now_map(g)) for g in range(groups)]
        + [
            pl.BlockSpec((taps, frame), const),
            pl.BlockSpec((2, owners, half), lambda b: (0, 0, 0)),
            pl.BlockSpec((per, half), const),
            pl.BlockSpec((per, half), const),
        ],
        out_specs=pl.BlockSpec((owners, WIDE * per, LANES), lambda b: (0, jnp.maximum(b - ahead, 0), 0)),
        out_shape=jax.ShapeDtypeStruct((owners, kept * per, LANES), jnp.float32),
        scratch_shapes=[
            pltpu.VMEM((owners * per, half), jnp.bfloat16),
            pltpu.VMEM((owners * per, half), jnp.bfloat16),
            pltpu.VMEM((taps - 1, groups, inputs, frame), jnp.float32),
            pltpu.VMEM((WIDE * LANES, half), jnp.bfloat16),
            pltpu.VMEM((WIDE * LANES, half), jnp.bfloat16),
        ],
        compiler_params=params(60),
        cost_estimate=pl.CostEstimate(
            flops=6 * owners * per * half * kept * LANES,
            bytes_accessed=4 * inputs * samples,
            transcendentals=0,
        ),
        name="first_chunk",
    )(*([voltages] * groups), fir_taps, outer, first, second)


def correlate_kernel(sizes, scale, places, *refs):
    tm_count, chan_count, blocks, per, inputs = sizes
    out_ref, token_ref, got_ref, sems = refs[-4:]
    groups = LANES // inputs
    channels = per // 2

    @pl.when(pl.program_id(0) == 0)
    def _():
        copies = []
        for index, (base, rows, into) in enumerate(places):
            source = refs[index].at[:, pl.ds(base, rows), :]
            target = got_ref.at[:, pl.ds(into, rows), :]
            copies.append(pltpu.make_async_copy(source, target, sems.at[index]))
            copies[-1].start()
        for copy in copies:
            copy.wait()
        token_ref[...] = jnp.zeros_like(token_ref)

    lane_group = lax.broadcasted_iota(jnp.int32, (blocks, LANES), 1) // inputs

    def piece(channel, time, chan, part):
        rows = pl.ds(part * channels + channel, blocks, stride=per)
        return got_ref[time * chan_count + chan, rows, :]

    def tile(channel, time, part, column):
        held = [piece(channel, time, column * groups + place, part) for place in range(groups)]
        made = []
        for group in range(groups):
            total = None
            for place in range(groups):
                turn = (place - group) * inputs % LANES
                value = pltpu.roll(held[place], turn, 1) if turn else held[place]
                total = value if total is None else jnp.where(lane_group == place, value, total)
            made.append(total)
        return jnp.concatenate(made, axis=0)

    def plane(channel, part):
        columns = []
        for column in range(chan_count // groups):
            columns.append(
                jnp.concatenate([tile(channel, time, part, column) for time in range(tm_count)], axis=0)
            )
        return jnp.concatenate(columns, axis=1)

    dot = functools.partial(lax.dot_general, dimension_numbers=NN, preferred_element_type=jnp.float32)
    for sub in range(PAIR):
        channel = pl.program_id(0) * PAIR + sub
        real, imag = plane(channel, 0), plane(channel, 1)
        real_high, real_low = halves(real)
        imag_high, imag_low = halves(imag)
        high = jnp.concatenate([real_high, imag_high], axis=0)
        low = jnp.concatenate([real_low, imag_low], axis=0)
        turned_high = jnp.concatenate([-imag_high, real_high], axis=0)
        turned_low = jnp.concatenate([-imag_low, real_low], axis=0)
        high_t, low_t = high.T, low.T
        for which, (other_high, other_low) in enumerate([(high, low), (turned_high, turned_low)]):
            total = dot(high_t, other_high) + dot(high_t, other_low) + dot(low_t, other_high)
            out_ref[sub, 0, which] = total * scale


def correlate_chunk(pieces, held, start, owned, sizes, spectra):
    tm_count, chan_count, blocks, per, inputs = sizes
    channels = per // 2
    everyone = chan_count * inputs
    owners = tm_count * chan_count
    operands = [piece[0] for piece in pieces]
    places = [piece[1:] for piece in pieces]
    aliases = {}
    if held is not None:
        aliases = {len(operands): 0}
        operands.append(held)
    return pl.pallas_call(
        functools.partial(correlate_kernel, sizes, 1.0 / spectra, places),
        grid=(channels // PAIR,),
        in_specs=[pl.BlockSpec(memory_space=pl.ANY)] * len(operands),
        out_specs=[
            pl.BlockSpec((PAIR, 1, 2, everyone, everyone), lambda c: (start // 2 // PAIR + c, start % 2, 0, 0, 0)),
            pl.BlockSpec((8, LANES), lambda c: (0, 0)),
        ],
        out_shape=[
            jax.ShapeDtypeStruct((owned // 2, 2, 2, everyone, everyone), jnp.float32),
            jax.ShapeDtypeStruct((8, LANES), jnp.float32),
        ],
        input_output_aliases=aliases,
        scratch_shapes=[
            pltpu.VMEM((owners, blocks * per, LANES), jnp.float32),
            pltpu.SemaphoreType.DMA((len(pieces),)),
        ],
        compiler_params=params(60),
        cost_estimate=pl.CostEstimate(
            flops=6 * channels * 2 * everyone * everyone * 2 * spectra,
            bytes_accessed=channels * 8 * everyone * everyone + 4 * owners * blocks * per * LANES,
            transcendentals=0,
        ),
        name="correlate_chunk",
    )(*operands)


def chunk_plan(owned):
    unit = owned // 8
    if owned % 32 == 0:
        return [[(0, 2 * unit)], [(2 * unit + 1, 3 * unit), (4 * unit, 2 * unit)], [(1, unit)]]
    return [[(parity, owned // 2)] for parity in (0, 1)]


def phases(frame, owners, owned, segments):
    samples = np.arange(frame // 2)
    outer = 2.0 * np.pi * ((np.arange(owners)[:, None] * owned * samples) % frame) / frame
    outer = np.stack([np.cos(outer), np.sin(outer)]).astype(np.float32)
    scale = 1.0 / np.sqrt(float(frame))
    tables = {}
    for start, count in segments:
        channels = start + 2 * np.arange(count)
        inner = 2.0 * np.pi * ((channels[:, None] * samples) % frame) / frame
        cosine, sine = np.cos(inner) * scale, np.sin(inner) * scale
        first = np.concatenate([cosine, -sine]).astype(np.float32)
        second = np.concatenate([-sine, -cosine]).astype(np.float32)
        tables[start, count] = (first, second)
    return outer, tables


def body(voltages, fir_taps):
    inputs, samples = voltages.shape
    taps, frame = fir_taps.shape
    spec_dev = samples // frame
    tm_count, chan_count = lax.axis_size("tm"), lax.axis_size("chan")
    owners = tm_count * chan_count
    owned = frame // 2 // owners
    groups = LANES // inputs
    blocks = spec_dev // groups
    chunks = chunk_plan(owned)
    outer, tables = phases(frame, owners, owned, sum(chunks, []))
    split = blocks > LATE and len(chunks) > 2

    def exchange(value):
        return lax.all_to_all(value, AXES, split_axis=0, concat_axis=0, tiled=True)

    halo = passed_along(voltages[:, samples - (taps - 1) * frame :], "tm", 1)
    if split:
        ahead = first_chunk(outer, *tables[chunks[0][0]], voltages, fir_taps, blocks, groups)
        ahead, halo = lax.optimization_barrier((ahead, halo))
    parts = filtered_parts(voltages, halo, fir_taps, blocks, groups)

    def transformed(segment, count, made, base, rows, token):
        return dft_chunk(
            outer, *tables[segment], *parts[segment[0] % 2], count, made, base, rows, token
        )

    pieces = {segment: [] for segment in sum(chunks, [])}
    out, token = None, None

    def correlate(segments):
        nonlocal out, token
        for segment in segments:
            start, count = segment
            sizes = (tm_count, chan_count, blocks, 2 * count, inputs)
            out, token = correlate_chunk(
                pieces[segment], out, start, owned, sizes, tm_count * spec_dev
            )

    for index, chunk in enumerate(chunks):
        if index == 0 and split:
            (segment,) = chunk
            per = 2 * segment[1]
            pieces[segment].append((exchange(ahead), 0, (blocks - LATE) * per, LATE * per))
            continue
        plan = [(segment, blocks) for segment in chunk]
        if index == 1 and split:
            plan.append((chunks[0][0], LATE))
        rows = sum(2 * segment[1] * count for segment, count in plan)
        made, base, places = None, 0, []
        for segment, count in plan:
            made = transformed(segment, count, made, base, rows, token)
            places.append((segment, base, 2 * segment[1] * count))
            base += 2 * segment[1] * count
        got = exchange(made)
        for segment, base, more in places:
            pieces[segment].append((got, base, more, 0))
    correlate(sum(chunks, []))
    return out.reshape(owned, 2, chan_count * inputs, chan_count * inputs)


def solution(mesh):
    placed = (P("chan", "tm"), P())
    return jax.shard_map(
        body,
        mesh=mesh,
        in_specs=placed,
        out_specs=P(("tm", "chan"), None, None, None),
        check_vma=False,
    )
```

time: 439 us -> 430 us (0.979)
  Pallas kernels: 154 us -> 123 us
  waiting for transfers between devices: 250 us -> 280 us
  local copies, waits for them, and re-layouts: 11.9 us -> 4.83 us
    all_to_all x4 -> x3, waiting for transfers between devices: 250 us -> 280 us  [exchange(): return lax.all_to_all(value, AXES, split_axis=0, concat_axis=0, tiled=True)]
    pallas_call x4, Pallas kernels: 66.9 us -> 43.1 us  [dft_chunk(): pl.pallas_call(functools.partial(dft_kernel, owners, per), grid=(blocks /...]
    pallas_call x4, Pallas kernels: 57.6 us -> 50.3 us  [correlate_chunk(): pl.pallas_call(functools.partial(correlate_kernel, sizes, 1.0 / spectra,...]
    unnamed x34 -> x6, local copies, waits for them, and re-layouts: 10.4 us -> 3.31 us
    all_to_all x4 -> x3, starting transfers between devices: 19.4 us -> 18.2 us  [exchange(): return lax.all_to_all(value, AXES, split_axis=0, concat_axis=0, tiled=True)]
  transfers between devices with their start and end apart: 5 -> 4, of which waited for: 3 -> 3; matrix products, arithmetic and copies ran while one was open for 0% -> 0% of each run, Pallas kernels for 34% -> 27%
where the time goes in v3:
time: 430 us; the launch traced here: 429 us
  waiting for transfers between devices  280 us (65%)
  Pallas kernels  123 us (29%)
  starting transfers between devices  20.7 us (5%)
  local copies, waits for them, and re-layouts  4.83 us (1%)
    all_to_all x3, waiting for transfers between devices, exchange(): return lax.all_to_all(value, AXES, split_axis=0, concat_axis=0, tiled=True)  280 us
    pallas_call x4, Pallas kernels, correlate_chunk(): pl.pallas_call(functools.partial(correlate_kernel, sizes, 1.0 / spectra,...  50.3 us
    pallas_call x4, Pallas kernels, dft_chunk(): pl.pallas_call(functools.partial(dft_kernel, owners, per), grid=(blocks /...  43.1 us
    all_to_all x3, starting transfers between devices, exchange(): return lax.all_to_all(value, AXES, split_axis=0, concat_axis=0, tiled=True)  18.2 us
    pallas_call x1, Pallas kernels, first_chunk(): pl.pallas_call(functools.partial(first_kernel, owners, per, taps, groups)...  15.1 us
    pallas_call x1, Pallas kernels, filtered_parts(): pl.pallas_call(functools.partial(filter_kernel, blocks, groups, taps), gr...  14.2 us
  transfers between devices with their start and end apart: 4, of which 3 were waited for; matrix products, arithmetic and copies ran while one was open for 0% of the time, Pallas kernels for 27%

profile of v3, /device:TPU:0, one launch (start us, length us, event | category | flops | bytes accessed | tf_op | source)
XLA Modules:
  0.0 429.0 jit_solution(2316252432830484776)
XLA Ops:
  0.0 1.5 slice.3
  1.5 2.5 collective-permute-start
  4.0 15.1 %first_chunk.1 = f32[32,160,128]{2,1,0:T(8,128)} custom-call(f32[64,65536]{1,0:T(8,128)} %volt_ref.1, f32[64,65536]{1,0:T(8,128)} %volt_ref.1, f32[4,2048]{1,0:T(4,128)} %fir_ref.1, f32[2,32,1024]{2,1,0:T(8,128)} %constant.18.clone.refs_3_.outer_ref, f32[16,1024]{1,0:T(8,128)} %constant.19.clone.refs_4_.first_ref, f32[16,1024]{1,0:T(8,128)} %constant.20.clone.refs_5_.second_ref), custom_call_target="tpu_custom_call" | custom-call | flops 4026531840 | bytes 16777216 | tf_op jit(solution)/shard_map/first_chunk/pallas_call | solution.py:273
  19.1 0.0 copy-start.1
  19.1 0.0 collective-permute-done.halo_ref
  19.1 11.6 %all-to-all-start.2 = ((f32[32,160,128]{2,1,0:T(8,128)}), f32[32,160,128]{2,1,0:T(8,128)}, u32[]{:S(2)}, u32[]{:S(2)}) async-start(f32[32,160,128]{2,1,0:T(8,128)} %first_chunk.1), calls=%async_computation.2 | async-start | bytes 5242880 | tf_op jit(solution)/shard_map/all_to_all | solution.py:437
  30.7 0.0 copy-done.1
  30.7 14.2 %polyphase_filter.1 = (bf16[16,2,64,1024]{3,2,1,0:T(8,128)(2,1)S(1)}, bf16[16,2,64,1024]{3,2,1,0:T(8,128)(2,1)}, bf16[16,2,64,1024]{3,2,1,0:T(8,128)(2,1)}, bf16[16,2,64,1024]{3,2,1,0:T(8,128)(2,1)}) custom-call(f32[64,65536]{1,0:T(8,128)} %volt_ref.1, f32[64,6144]{1,0:T(8,128)S(1)} %collective-permute-done.halo_ref, f32[4,2048]{1,0:T(4,128)S(1)} %copy-done.1), custom_call_target="tpu_custom_call" | custom-call | flops 33554432 | bytes 33554432 | tf_op jit(solution)/shard_map/polyphase_filter/pallas_call | solution.py:89
  44.9 0.0 copy-start
  44.9 2.0 copy-done
  46.9 14.8 %dft_chunk.5.rest_0_ = f32[32,736,128]{2,1,0:T(8,128)} custom-call(f32[2,32,1024]{2,1,0:T(8,128)} %constant.18.clone.refs_3_.outer_ref, f32[24,1024]{1,0:T(8,128)} %constant.21.clone.first_ref, f32[24,1024]{1,0:T(8,128)} %constant.22.clone.second_ref, bf16[2048,1024]{1,0:T(8,128)(2,1)} %bitcast.9, bf16[2048,1024]{1,0:T(8,128)(2,1)} %bitcast.11), custom_call_target="tpu_custom_call" | custom-call | flops 9663676416 | bytes 14680064 | tf_op jit(solution)/shard_map/dft_chunk/pallas_call | solution.py:170
  61.7 12.4 %dft_chunk.6.rest_0_ = f32[32,736,128]{2,1,0:T(8,128)} custom-call(f32[2,32,1024]{2,1,0:T(8,128)} %constant.18.clone.refs_3_.outer_ref, f32[16,1024]{1,0:T(8,128)} %constant.23.clone.first_ref, f32[16,1024]{1,0:T(8,128)} %constant.24.clone.second_ref, bf16[2048,1024]{1,0:T(8,128)(2,1)} %bitcast.5, ...), custom_call_target="tpu_custom_call", output_to_operand_aliasing={{}: (5, {})} | custom-call | flops 6442450944 | bytes 12582912 | tf_op jit(solution)/shard_map/dft_chunk/pallas_call | solution.py:170
  74.0 6.3 %dft_chunk.7 = f32[32,736,128]{2,1,0:T(8,128)} custom-call(f32[2,32,1024]{2,1,0:T(8,128)} %constant.18.clone.refs_3_.outer_ref, f32[16,1024]{1,0:T(8,128)} %constant.19.clone.refs_4_.first_ref, f32[16,1024]{1,0:T(8,128)} %constant.20.clone.refs_5_.second_ref, bf16[2048,1024]{1,0:T(8,128)(2,1)} %bitcast.6, ...), custom_call_target="tpu_custom_call", output_to_operand_aliasing={{}: (5, {})} | custom-call | flops 2415919104 | bytes 4718592 | tf_op jit(solution)/shard_map/dft_chunk/pallas_call | solution.py:170
  80.3 12.0 %all-to-all-done.2.refs_0_ = f32[32,160,128]{2,1,0:T(8,128)} async-done(((f32[32,160,128]{2,1,0:T(8,128)}), f32[32,160,128]{2,1,0:T(8,128)}, u32[]{:S(2)}, u32[]{:S(2)}) %all-to-all-start.2) | async-done | bytes 2621472 | tf_op jit(solution)/shard_map/all_to_all | solution.py:437
  92.3 3.8 all-to-all-start.1
  96.1 9.7 %dft_chunk.4 = f32[32,128,128]{2,1,0:T(8,128)} custom-call(f32[2,32,1024]{2,1,0:T(8,128)} %constant.18.clone.refs_3_.outer_ref, f32[8,1024]{1,0:T(8,128)} %constant.25.clone.first_ref, f32[8,1024]{1,0:T(8,128)} %constant.26.clone.second_ref, bf16[2048,1024]{1,0:T(8,128)(2,1)} %bitcast.10, bf16[2048,1024]{1,0:T(8,128)(2,1)} %bitcast.12), custom_call_target="tpu_custom_call" | custom-call | flops 3221225472 | bytes 10485760 | tf_op jit(solution)/shard_map/dft_chunk/pallas_call | solution.py:170
  105.8 261.2 %all-to-all-done.1.refs_1_.refs_0_ = f32[32,736,128]{2,1,0:T(8,128)} async-done(((f32[32,736,128]{2,1,0:T(8,128)}), f32[32,736,128]{2,1,0:T(8,128)}, u32[]{:S(2)}, u32[]{:S(2)}) %all-to-all-start.1) | async-done | bytes 12058656 | tf_op jit(solution)/shard_map/all_to_all | solution.py:437
  367.0 2.9 all-to-all-start
  369.9 12.9 %correlate_chunk.4 = (f32[16,2,2,512,512]{4,3,2,1,0:T(8,128)}, f32[8,128]{1,0:T(8,128)}) custom-call(f32[32,160,128]{2,1,0:T(8,128)} %all-to-all-done.2.refs_0_, f32[32,736,128]{2,1,0:T(8,128)} %all-to-all-done.1.refs_1_.refs_0_), custom_call_target="tpu_custom_call" | custom-call | flops 6442450944 | bytes 20971520 | tf_op jit(solution)/shard_map/correlate_chunk/pallas_call | solution.py:373
  382.9 16.9 %correlate_chunk.5 = (f32[16,2,2,512,512]{4,3,2,1,0:T(8,128)}, f32[8,128]{1,0:T(8,128)}) custom-call(f32[32,736,128]{2,1,0:T(8,128)} %all-to-all-done.1.refs_1_.refs_0_, f32[16,2,2,512,512]{4,3,2,1,0:T(8,128)} %get-tuple-element.21.refs_1_), custom_call_target="tpu_custom_call", output_to_operand_aliasing={{0}: (1, {})} | custom-call | flops 9663676416 | bytes 31457280 | tf_op jit(solution)/shard_map/correlate_chunk/pallas_call | solution.py:373
  399.7 12.9 %correlate_chunk.6 = (f32[16,2,2,512,512]{4,3,2,1,0:T(8,128)}, f32[8,128]{1,0:T(8,128)}) custom-call(f32[32,736,128]{2,1,0:T(8,128)} %all-to-all-done.1.refs_1_.refs_0_, f32[16,2,2,512,512]{4,3,2,1,0:T(8,128)} %get-tuple-element.22.refs_1_), custom_call_target="tpu_custom_call", output_to_operand_aliasing={{0}: (1, {})} | custom-call | flops 6442450944 | bytes 20971520 | tf_op jit(solution)/shard_map/correlate_chunk/pallas_call | solution.py:373
  412.6 7.2 %all-to-all-done.refs_0_ = f32[32,128,128]{2,1,0:T(8,128)S(1)} async-done(((f32[32,128,128]{2,1,0:T(8,128)}), f32[32,128,128]{2,1,0:T(8,128)S(1)}, u32[]{:S(2)}, u32[]{:S(2)}) %all-to-all-start) | async-done | bytes 2097184 | tf_op jit(solution)/shard_map/all_to_all | solution.py:437
  419.8 0.0 copy-start.2
  419.8 1.3 copy-done.2
  421.2 7.6 %correlate_chunk.7 = (f32[16,2,2,512,512]{4,3,2,1,0:T(8,128)}, f32[8,128]{1,0:T(8,128)}) custom-call(f32[32,128,128]{2,1,0:T(8,128)} %copy-done.2, f32[16,2,2,512,512]{4,3,2,1,0:T(8,128)} %get-tuple-element.23.refs_1_), custom_call_target="tpu_custom_call", output_to_operand_aliasing={{0}: (1, {})} | custom-call | flops 3221225472 | bytes 10485760 | tf_op jit(solution)/shard_map/correlate_chunk/pallas_call | solution.py:373
Async XLA Ops:
  1.5 17.6 %collective-permute-start = (f32[64,6144]{1,0:T(8,128)S(1)}, f32[64,6144]{1,0:T(8,128)S(1)}, u32[]{:S(2)}, u32[]{:S(2)}) collective-permute-start(f32[64,6144]{1,0:T(8,128)S(1)} %slice.3), channel_id=1, source_target_pairs={{0,8},{8,16},{16,24},{1,9},{9,17},{17,25},{2,10},{10,18},{18,26},{... | collective-permute-start | bytes 4718600 | tf_op jit(solution)/shard_map/ppermute | solution.py:34
  19.1 11.6 %copy-start.1 = (f32[4,2048]{1,0:T(4,128)S(1)}, f32[4,2048]{1,0:T(4,128)}, u32[]{:S(2)}) copy-start(f32[4,2048]{1,0:T(4,128)} %fir_ref.1) | copy-start | bytes 98308
  19.1 73.2 %all-to-all-start.2 = ((f32[32,160,128]{2,1,0:T(8,128)}), f32[32,160,128]{2,1,0:T(8,128)}, u32[]{:S(2)}, u32[]{:S(2)}) async-start(f32[32,160,128]{2,1,0:T(8,128)} %first_chunk.1), calls=%async_computation.2 | async-start | bytes 5242880 | tf_op jit(solution)/shard_map/all_to_all | solution.py:437
  44.9 2.0 copy-start
  92.3 274.7 %all-to-all-start.1 = ((f32[32,736,128]{2,1,0:T(8,128)}), f32[32,736,128]{2,1,0:T(8,128)}, u32[]{:S(2)}, u32[]{:S(2)}) async-start(f32[32,736,128]{2,1,0:T(8,128)} %dft_chunk.7), calls=%async_computation.1 | async-start | bytes 24117248 | tf_op jit(solution)/shard_map/all_to_all | solution.py:437
  367.0 52.8 %all-to-all-start = ((f32[32,128,128]{2,1,0:T(8,128)}), f32[32,128,128]{2,1,0:T(8,128)S(1)}, u32[]{:S(2)}, u32[]{:S(2)}) async-start(f32[32,128,128]{2,1,0:T(8,128)} %dft_chunk.4), calls=%async_computation | async-start | bytes 4194304 | tf_op jit(solution)/shard_map/all_to_all | solution.py:437
  419.8 1.3 copy-start.2

commit v4 on v3

--- a/solution.py
+++ b/solution.py
@@ -96,7 +96,7 @@
         ],
         out_specs=[out_spec] * 4,
         out_shape=[shape] * 4,
-        compiler_params=params(48),
+        compiler_params=params(60),
         cost_estimate=pl.CostEstimate(
             flops=8 * inputs * samples, bytes_accessed=8 * inputs * samples, transcendentals=0
         ),
@@ -129,7 +129,7 @@
 def transform(owners, per, table_high, table_low, high, low, out_ref):
     dot = functools.partial(lax.dot_general, dimension_numbers=NT, preferred_element_type=jnp.float32)
     total = dot(table_high[...], high) + dot(table_high[...], low) + dot(table_low[...], high)
-    for block in range(WIDE):
+    for block in range(high.shape[0] // LANES):
         part = total[:, block * LANES : (block + 1) * LANES]
         out_ref[:, block * per : (block + 1) * per, :] = part.reshape(owners, per, LANES)
 
@@ -147,9 +147,10 @@
 def dft_chunk(outer, first, second, high, low, blocks, held, base, total_rows, token=None):
     per, frame = first.shape
     owners = outer.shape[1]
-    rows = WIDE * LANES
-    assert base % (WIDE * per) == 0
-    skip = base // (WIDE * per)
+    wide = 2 * WIDE if blocks % (2 * WIDE) == 0 and base % (2 * WIDE * per) == 0 else WIDE
+    rows = wide * LANES
+    assert base % (wide * per) == 0
+    skip = base // (wide * per)
     const = lambda b: (0, 0)
     operands = [outer, first, second, high, low]
     in_specs = [
@@ -169,9 +170,9 @@
         in_specs.append(pl.BlockSpec(memory_space=pl.ANY))
     return pl.pallas_call(
         functools.partial(dft_kernel, owners, per),
-        grid=(blocks // WIDE,),
+        grid=(blocks // wide,),
         in_specs=in_specs,
-        out_specs=pl.BlockSpec((owners, WIDE * per, LANES), lambda b: (0, skip + b, 0)),
+        out_specs=pl.BlockSpec((owners, wide * per, LANES), lambda b: (0, skip + b, 0)),
         out_shape=jax.ShapeDtypeStruct((owners, total_rows, LANES), jnp.float32),
         input_output_aliases=aliases,
         scratch_shapes=[
@@ -301,21 +302,27 @@
 
 def correlate_kernel(sizes, scale, places, *refs):
     tm_count, chan_count, blocks, per, inputs = sizes
-    out_ref, token_ref, got_ref, sems = refs[-4:]
     groups = LANES // inputs
     channels = per // 2
+    if places is None:
+        got_ref, (out_ref, token_ref) = refs[0], refs[-2:]
+    else:
+        out_ref, token_ref, got_ref, sems = refs[-4:]
+
+    @pl.when(pl.program_id(0) == 0)
+    def _():
+        token_ref[...] = jnp.zeros_like(token_ref)
 
     @pl.when(pl.program_id(0) == 0)
     def _():
         copies = []
-        for index, (base, rows, into) in enumerate(places):
+        for index, (base, rows, into) in enumerate(places or []):
             source = refs[index].at[:, pl.ds(base, rows), :]
             target = got_ref.at[:, pl.ds(into, rows), :]
             copies.append(pltpu.make_async_copy(source, target, sems.at[index]))
             copies[-1].start()
         for copy in copies:
             copy.wait()
-        token_ref[...] = jnp.zeros_like(token_ref)
 
     lane_group = lax.broadcasted_iota(jnp.int32, (blocks, LANES), 1) // inputs
 
@@ -366,14 +373,24 @@
     owners = tm_count * chan_count
     operands = [piece[0] for piece in pieces]
     places = [piece[1:] for piece in pieces]
+    in_specs = [pl.BlockSpec(memory_space=pl.ANY)] * len(operands)
+    limit = 60
+    scratch = [
+        pltpu.VMEM((owners, blocks * per, LANES), jnp.float32),
+        pltpu.SemaphoreType.DMA((len(pieces),)),
+    ]
+    if len(pieces) == 1 and operands[0].shape[1] == blocks * per and per <= 8:
+        places, scratch, limit = None, [], 40
+        in_specs = [pl.BlockSpec(operands[0].shape, lambda c: (0, 0, 0))]
     aliases = {}
     if held is not None:
         aliases = {len(operands): 0}
         operands.append(held)
+        in_specs.append(pl.BlockSpec(memory_space=pl.ANY))
     return pl.pallas_call(
         functools.partial(correlate_kernel, sizes, 1.0 / spectra, places),
         grid=(channels // PAIR,),
-        in_specs=[pl.BlockSpec(memory_space=pl.ANY)] * len(operands),
+        in_specs=in_specs,
         out_specs=[
             pl.BlockSpec((PAIR, 1, 2, everyone, everyone), lambda c: (start // 2 // PAIR + c, start % 2, 0, 0, 0)),
             pl.BlockSpec((8, LANES), lambda c: (0, 0)),
@@ -383,11 +400,8 @@
             jax.ShapeDtypeStruct((8, LANES), jnp.float32),
         ],
         input_output_aliases=aliases,
-        scratch_shapes=[
-            pltpu.VMEM((owners, blocks * per, LANES), jnp.float32),
-            pltpu.SemaphoreType.DMA((len(pieces),)),
-        ],
-        compiler_params=params(60),
+        scratch_shapes=scratch,
+        compiler_params=params(limit),
         cost_estimate=pl.CostEstimate(
             flops=6 * channels * 2 * everyone * everyone * 2 * spectra,
             bytes_accessed=channels * 8 * everyone * everyone + 4 * owners * blocks * per * LANES,
@@ -459,6 +473,7 @@
                 pieces[segment], out, start, owned, sizes, tm_count * spec_dev
             )
 
+    payloads, layouts = [], []
     for index, chunk in enumerate(chunks):
         if index == 0 and split:
             (segment,) = chunk
@@ -474,6 +489,10 @@
             made = transformed(segment, count, made, base, rows, token)
             places.append((segment, base, 2 * segment[1] * count))
             base += 2 * segment[1] * count
+        payloads.append(made)
+        layouts.append(places)
+    payloads = lax.optimization_barrier(tuple(payloads))
+    for made, places in zip(payloads, layouts):
         got = exchange(made)
         for segment, base, more in places:
             pieces[segment].append((got, base, more, 0))

time: 430 us -> 419 us (0.974)
  blocking collectives: 0 us -> 268 us
  waiting for transfers between devices: 280 us -> 13.9 us
    all_to_all x0 -> x1, blocking collectives: none -> 268 us  [exchange(): return lax.all_to_all(value, AXES, split_axis=0, concat_axis=0, tiled=True)]
    all_to_all x3 -> x2, waiting for transfers between devices: 280 us -> 13.9 us  [exchange(): return lax.all_to_all(value, AXES, split_axis=0, concat_axis=0, tiled=True)]
    all_to_all x3 -> x2, starting transfers between devices: 18.2 us -> 13.4 us  [exchange(): return lax.all_to_all(value, AXES, split_axis=0, concat_axis=0, tiled=True)]
  transfers between devices with their start and end apart: 4 -> 3, of which waited for: 3 -> 2; matrix products, arithmetic and copies ran while one was open for 0% -> 0% of each run, Pallas kernels for 27% -> 27%
where the time goes in v4:
time: 419 us
  blocking collectives  268 us (64%)
  Pallas kernels  119 us (28%)
  starting transfers between devices  17 us (4%)
  waiting for transfers between devices  13.9 us (3%)
    all_to_all x1, blocking collectives, exchange(): return lax.all_to_all(value, AXES, split_axis=0, concat_axis=0, tiled=True)  268 us
    pallas_call x4, Pallas kernels, correlate_chunk(): pl.pallas_call(functools.partial(correlate_kernel, sizes, 1.0 / spectra,...  48.7 us
    pallas_call x4, Pallas kernels, dft_chunk(): pl.pallas_call(functools.partial(dft_kernel, owners, per), grid=(blocks /...  39.2 us
    pallas_call x1, Pallas kernels, filtered_parts(): pl.pallas_call(functools.partial(filter_kernel, blocks, groups, taps), gr...  15.8 us
    pallas_call x1, Pallas kernels, first_chunk(): pl.pallas_call(functools.partial(first_kernel, owners, per, taps, groups)...  15.1 us
    all_to_all x2, waiting for transfers between devices, exchange(): return lax.all_to_all(value, AXES, split_axis=0, concat_axis=0, tiled=True)  13.9 us
    all_to_all x2, starting transfers between devices, exchange(): return lax.all_to_all(value, AXES, split_axis=0, concat_axis=0, tiled=True)  13.4 us
  transfers between devices with their start and end apart: 3, of which 2 were waited for; matrix products, arithmetic and copies ran while one was open for 0% of the time, Pallas kernels for 27%

profile of v4, /device:TPU:0, one launch (start us, length us, event | category | flops | bytes accessed | tf_op | source)
XLA Modules:
  0.0 418.7 jit_solution(14420530567180144621)
XLA Ops:
  0.0 1.5 slice.3
  1.5 3.5 collective-permute-start
  5.1 15.1 %first_chunk.1 = f32[32,160,128]{2,1,0:T(8,128)} custom-call(f32[64,65536]{1,0:T(8,128)} %volt_ref.1, f32[64,65536]{1,0:T(8,128)} %volt_ref.1, f32[4,2048]{1,0:T(4,128)} %fir_ref.1, f32[2,32,1024]{2,1,0:T(8,128)} %constant.18.clone.refs_3_.outer_ref, f32[16,1024]{1,0:T(8,128)} %constant.19.clone.refs_4_.first_ref, f32[16,1024]{1,0:T(8,128)} %constant.20.clone.refs_5_.second_ref), custom_call_target="tpu_custom_call" | custom-call | flops 4026531840 | bytes 16777216 | tf_op jit(solution)/shard_map/first_chunk/pallas_call | solution.py:274
  20.1 0.0 collective-permute-done.halo_ref
  20.1 10.5 %all-to-all-start.2 = ((f32[32,160,128]{2,1,0:T(8,128)}), f32[32,160,128]{2,1,0:T(8,128)S(1)}, u32[]{:S(2)}, u32[]{:S(2)}) async-start(f32[32,160,128]{2,1,0:T(8,128)} %first_chunk.1), calls=%async_computation.2 | async-start | bytes 5242880 | tf_op jit(solution)/shard_map/all_to_all | solution.py:451
  30.7 15.8 %polyphase_filter.1 = (bf16[16,2,64,1024]{3,2,1,0:T(8,128)(2,1)}, bf16[16,2,64,1024]{3,2,1,0:T(8,128)(2,1)}, bf16[16,2,64,1024]{3,2,1,0:T(8,128)(2,1)}, bf16[16,2,64,1024]{3,2,1,0:T(8,128)(2,1)}) custom-call(f32[64,65536]{1,0:T(8,128)} %volt_ref.1, f32[64,6144]{1,0:T(8,128)} %collective-permute-done.halo_ref, f32[4,2048]{1,0:T(4,128)} %fir_ref.1), custom_call_target="tpu_custom_call" | custom-call | flops 33554432 | bytes 33554432 | tf_op jit(solution)/shard_map/polyphase_filter/pallas_call | solution.py:89
  46.4 14.3 %dft_chunk.4.rest_0_ = f32[32,736,128]{2,1,0:T(8,128)} custom-call(f32[2,32,1024]{2,1,0:T(8,128)} %constant.18.clone.refs_3_.outer_ref, f32[24,1024]{1,0:T(8,128)} %constant.21.clone.first_ref, f32[24,1024]{1,0:T(8,128)} %constant.22.clone.second_ref, bf16[2048,1024]{1,0:T(8,128)(2,1)} %bitcast.9, bf16[2048,1024]{1,0:T(8,128)(2,1)} %bitcast.11), custom_call_target="tpu_custom_call" | custom-call | flops 9663676416 | bytes 14680064 | tf_op jit(solution)/shard_map/dft_chunk/pallas_call | solution.py:171
  60.8 10.8 %dft_chunk.5.rest_0_ = f32[32,736,128]{2,1,0:T(8,128)} custom-call(f32[2,32,1024]{2,1,0:T(8,128)} %constant.18.clone.refs_3_.outer_ref, f32[16,1024]{1,0:T(8,128)} %constant.23.clone.first_ref, f32[16,1024]{1,0:T(8,128)} %constant.24.clone.second_ref, bf16[2048,1024]{1,0:T(8,128)(2,1)} %bitcast.5, ...), custom_call_target="tpu_custom_call", output_to_operand_aliasing={{}: (5, {})} | custom-call | flops 6442450944 | bytes 12582912 | tf_op jit(solution)/shard_map/dft_chunk/pallas_call | solution.py:171
  71.5 6.3 %dft_chunk.6 = f32[32,736,128]{2,1,0:T(8,128)} custom-call(f32[2,32,1024]{2,1,0:T(8,128)} %constant.18.clone.refs_3_.outer_ref, f32[16,1024]{1,0:T(8,128)} %constant.19.clone.refs_4_.first_ref, f32[16,1024]{1,0:T(8,128)} %constant.20.clone.refs_5_.second_ref, bf16[2048,1024]{1,0:T(8,128)(2,1)} %bitcast.6, ...), custom_call_target="tpu_custom_call", output_to_operand_aliasing={{}: (5, {})} | custom-call | flops 2415919104 | bytes 4718592 | tf_op jit(solution)/shard_map/dft_chunk/pallas_call | solution.py:171
  77.8 7.8 %dft_chunk.7 = f32[32,128,128]{2,1,0:T(8,128)} custom-call(f32[2,32,1024]{2,1,0:T(8,128)} %constant.18.clone.refs_3_.outer_ref, f32[8,1024]{1,0:T(8,128)} %constant.25.clone.first_ref, f32[8,1024]{1,0:T(8,128)} %constant.26.clone.second_ref, bf16[2048,1024]{1,0:T(8,128)(2,1)} %bitcast.10, bf16[2048,1024]{1,0:T(8,128)(2,1)} %bitcast.12), custom_call_target="tpu_custom_call" | custom-call | flops 3221225472 | bytes 10485760 | tf_op jit(solution)/shard_map/dft_chunk/pallas_call | solution.py:171
  85.6 6.7 %all-to-all-done.2.refs_0_ = f32[32,160,128]{2,1,0:T(8,128)S(1)} async-done(((f32[32,160,128]{2,1,0:T(8,128)}), f32[32,160,128]{2,1,0:T(8,128)S(1)}, u32[]{:S(2)}, u32[]{:S(2)}) %all-to-all-start.2) | async-done | bytes 2621472 | tf_op jit(solution)/shard_map/all_to_all | solution.py:451
  92.3 0.0 copy-start
  92.3 267.5 %all_to_all.15.refs_1_.refs_0_ = f32[32,736,128]{2,1,0:T(8,128)} all-to-all(f32[32,736,128]{2,1,0:T(8,128)} %dft_chunk.6), channel_id=1, replica_groups=mesh['tm'=4,'chan'=8] {'tm','chan'}, dimensions={0} | all-to-all | bytes 24117248 | tf_op jit(solution)/shard_map/all_to_all | solution.py:451
  359.8 0.0 copy-done
  359.8 2.9 all-to-all-start
  362.7 12.9 %correlate_chunk.4 = (f32[16,2,2,512,512]{4,3,2,1,0:T(8,128)}, f32[8,128]{1,0:T(8,128)}) custom-call(f32[32,160,128]{2,1,0:T(8,128)} %copy-done, f32[32,736,128]{2,1,0:T(8,128)} %all_to_all.15.refs_1_.refs_0_), custom_call_target="tpu_custom_call" | custom-call | flops 6442450944 | bytes 20971520 | tf_op jit(solution)/shard_map/correlate_chunk/pallas_call | solution.py:390
  375.7 16.8 %correlate_chunk.5 = (f32[16,2,2,512,512]{4,3,2,1,0:T(8,128)}, f32[8,128]{1,0:T(8,128)}) custom-call(f32[32,736,128]{2,1,0:T(8,128)} %all_to_all.15.refs_1_.refs_0_, f32[16,2,2,512,512]{4,3,2,1,0:T(8,128)} %get-tuple-element.25.refs_1_), custom_call_target="tpu_custom_call", output_to_operand_aliasing={{0}: (1, {})} | custom-call | flops 9663676416 | bytes 31457280 | tf_op jit(solution)/shard_map/correlate_chunk/pallas_call | solution.py:390
  392.5 12.9 %correlate_chunk.6 = (f32[16,2,2,512,512]{4,3,2,1,0:T(8,128)}, f32[8,128]{1,0:T(8,128)}) custom-call(f32[32,736,128]{2,1,0:T(8,128)} %all_to_all.15.refs_1_.refs_0_, f32[16,2,2,512,512]{4,3,2,1,0:T(8,128)} %get-tuple-element.26.refs_1_), custom_call_target="tpu_custom_call", output_to_operand_aliasing={{0}: (1, {})} | custom-call | flops 6442450944 | bytes 20971520 | tf_op jit(solution)/shard_map/correlate_chunk/pallas_call | solution.py:390
  405.4 7.2 %all-to-all-done.refs_0_ = f32[32,128,128]{2,1,0:T(8,128)S(1)} async-done(((f32[32,128,128]{2,1,0:T(8,128)}), f32[32,128,128]{2,1,0:T(8,128)S(1)}, u32[]{:S(2)}, u32[]{:S(2)}) %all-to-all-start) | async-done | bytes 2097184 | tf_op jit(solution)/shard_map/all_to_all | solution.py:451
  412.7 6.0 %correlate_chunk.7 = (f32[16,2,2,512,512]{4,3,2,1,0:T(8,128)}, f32[8,128]{1,0:T(8,128)}) custom-call(f32[32,128,128]{2,1,0:T(8,128)S(1)} %all-to-all-done.refs_0_, f32[16,2,2,512,512]{4,3,2,1,0:T(8,128)} %get-tuple-element.27.refs_1_), custom_call_target="tpu_custom_call", output_to_operand_aliasing={{0}: (1, {})} | custom-call | flops 3221225472 | bytes 10485760 | tf_op jit(solution)/shard_map/correlate_chunk/pallas_call | solution.py:390
Async XLA Ops:
  1.5 18.6 %collective-permute-start = (f32[64,6144]{1,0:T(8,128)S(1)}, f32[64,6144]{1,0:T(8,128)}, u32[]{:S(2)}, u32[]{:S(2)}) collective-permute-start(f32[64,6144]{1,0:T(8,128)S(1)} %slice.3), channel_id=1, source_target_pairs={{0,8},{8,16},{16,24},{1,9},{9,17},{17,25},{2,10},{10,18},{18,26},{... | collective-permute-start | bytes 4718600 | tf_op jit(solution)/shard_map/ppermute | solution.py:34
  20.1 72.2 %all-to-all-start.2 = ((f32[32,160,128]{2,1,0:T(8,128)}), f32[32,160,128]{2,1,0:T(8,128)S(1)}, u32[]{:S(2)}, u32[]{:S(2)}) async-start(f32[32,160,128]{2,1,0:T(8,128)} %first_chunk.1), calls=%async_computation.2 | async-start | bytes 5242880 | tf_op jit(solution)/shard_map/all_to_all | solution.py:451
  92.3 267.5 %copy-start = (f32[32,160,128]{2,1,0:T(8,128)}, f32[32,160,128]{2,1,0:T(8,128)S(1)}, u32[]{:S(2)}) copy-start(f32[32,160,128]{2,1,0:T(8,128)S(1)} %all-to-all-done.2.refs_0_) | copy-start | bytes 7864324
  359.8 52.8 %all-to-all-start = ((f32[32,128,128]{2,1,0:T(8,128)}), f32[32,128,128]{2,1,0:T(8,128)S(1)}, u32[]{:S(2)}, u32[]{:S(2)}) async-start(f32[32,128,128]{2,1,0:T(8,128)} %dft_chunk.7), calls=%async_computation | async-start | bytes 4194304 | tf_op jit(solution)/shard_map/all_to_all | solution.py:451

commit v5 on v4

--- a/solution.py
+++ b/solution.py
@@ -98,7 +98,7 @@
         out_shape=[shape] * 4,
         compiler_params=params(60),
         cost_estimate=pl.CostEstimate(
-            flops=8 * inputs * samples, bytes_accessed=8 * inputs * samples, transcendentals=0
+            flops=8000 * inputs * samples, bytes_accessed=8 * inputs * samples, transcendentals=0
         ),
         name="polyphase_filter",
     )(voltages, halo, fir_taps)
@@ -181,7 +181,7 @@
         ],
         compiler_params=params(60),
         cost_estimate=pl.CostEstimate(
-            flops=6 * owners * per * frame * blocks * LANES,
+            flops=60 * owners * per * frame * blocks * LANES,
             bytes_accessed=4 * blocks * LANES * frame + 4 * owners * blocks * per * LANES,
             transcendentals=0,
         ),
@@ -453,7 +453,6 @@
     halo = passed_along(voltages[:, samples - (taps - 1) * frame :], "tm", 1)
     if split:
         ahead = first_chunk(outer, *tables[chunks[0][0]], voltages, fir_taps, blocks, groups)
-        ahead, halo = lax.optimization_barrier((ahead, halo))
     parts = filtered_parts(voltages, halo, fir_taps, blocks, groups)
 
     def transformed(segment, count, made, base, rows, token):

time: 419 us -> 415 us (level)
  starting transfers between devices: 17 us -> 12.5 us
where the time goes in v5:
time: 415 us; the launch traced here: 414 us
  blocking collectives  267 us (64%)
  Pallas kernels  119 us (29%)
  waiting for transfers between devices  12.7 us (3%)
  starting transfers between devices  12.5 us (3%)
    all_to_all x1, blocking collectives, exchange(): return lax.all_to_all(value, AXES, split_axis=0, concat_axis=0, tiled=True)  267 us
    pallas_call x4, Pallas kernels, correlate_chunk(): pl.pallas_call(functools.partial(correlate_kernel, sizes, 1.0 / spectra,...  48.7 us
    pallas_call x4, Pallas kernels, dft_chunk(): pl.pallas_call(functools.partial(dft_kernel, owners, per), grid=(blocks /...  39.2 us
    pallas_call x1, Pallas kernels, filtered_parts(): pl.pallas_call(functools.partial(filter_kernel, blocks, groups, taps), gr...  15.7 us
    pallas_call x1, Pallas kernels, first_chunk(): pl.pallas_call(functools.partial(first_kernel, owners, per, taps, groups)...  15.1 us
    all_to_all x2, waiting for transfers between devices, exchange(): return lax.all_to_all(value, AXES, split_axis=0, concat_axis=0, tiled=True)  12.7 us
    all_to_all x2, starting transfers between devices, exchange(): return lax.all_to_all(value, AXES, split_axis=0, concat_axis=0, tiled=True)  10 us
  transfers between devices with their start and end apart: 3, of which 2 were waited for; matrix products, arithmetic and copies ran while one was open for 0% of the time, Pallas kernels for 27%

profile of v5, /device:TPU:0, one launch (start us, length us, event | category | flops | bytes accessed | tf_op | source)
XLA Modules:
  0.0 413.9 jit_solution(9782128253133996995)
XLA Ops:
  0.0 1.5 slice.3
  1.5 2.5 collective-permute-start
  4.0 15.1 %first_chunk.1 = f32[32,160,128]{2,1,0:T(8,128)} custom-call(f32[64,65536]{1,0:T(8,128)} %refs_1_.1, f32[64,65536]{1,0:T(8,128)} %refs_1_.1, f32[4,2048]{1,0:T(4,128)} %refs_2_.1, f32[2,32,1024]{2,1,0:T(8,128)} %constant.18.clone.outer_ref.refs_3_, f32[16,1024]{1,0:T(8,128)} %constant.19.clone.first_ref.refs_4_, f32[16,1024]{1,0:T(8,128)} %constant.20.clone.second_ref.refs_5_), custom_call_target="tpu_custom_call" | custom-call | flops 4026531840 | bytes 16777216 | tf_op jit(solution)/shard_map/first_chunk/pallas_call | solution.py:274
  19.1 7.1 %all-to-all-start.2 = ((f32[32,160,128]{2,1,0:T(8,128)}), f32[32,160,128]{2,1,0:T(8,128)}, u32[]{:S(2)}, u32[]{:S(2)}) async-start(f32[32,160,128]{2,1,0:T(8,128)} %first_chunk.1), calls=%async_computation.2 | async-start | bytes 5242880 | tf_op jit(solution)/shard_map/all_to_all | solution.py:451
  26.2 0.0 collective-permute-done.halo_ref
  26.2 0.0 copy-start
  26.2 1.1 copy-done
  27.4 15.7 %polyphase_filter.1 = (bf16[16,2,64,1024]{3,2,1,0:T(8,128)(2,1)}, bf16[16,2,64,1024]{3,2,1,0:T(8,128)(2,1)}, bf16[16,2,64,1024]{3,2,1,0:T(8,128)(2,1)}, bf16[16,2,64,1024]{3,2,1,0:T(8,128)(2,1)}) custom-call(f32[64,65536]{1,0:T(8,128)} %refs_1_.1, f32[64,6144]{1,0:T(8,128)} %copy-done, f32[4,2048]{1,0:T(4,128)} %refs_2_.1), custom_call_target="tpu_custom_call" | custom-call | flops 33554432000 | bytes 33554432 | tf_op jit(solution)/shard_map/polyphase_filter/pallas_call | solution.py:89
  43.1 14.3 %dft_chunk.4.rest_0_ = f32[32,736,128]{2,1,0:T(8,128)} custom-call(f32[2,32,1024]{2,1,0:T(8,128)} %constant.18.clone.outer_ref.refs_3_, f32[24,1024]{1,0:T(8,128)} %constant.21.clone.first_ref, f32[24,1024]{1,0:T(8,128)} %constant.22.clone.second_ref, bf16[2048,1024]{1,0:T(8,128)(2,1)} %bitcast.5, bf16[2048,1024]{1,0:T(8,128)(2,1)} %bitcast.7), custom_call_target="tpu_custom_call" | custom-call | flops 96636764160 | bytes 14680064 | tf_op jit(solution)/shard_map/dft_chunk/pallas_call | solution.py:171
  57.4 10.8 %dft_chunk.5.rest_0_ = f32[32,736,128]{2,1,0:T(8,128)} custom-call(f32[2,32,1024]{2,1,0:T(8,128)} %constant.18.clone.outer_ref.refs_3_, f32[16,1024]{1,0:T(8,128)} %constant.23.clone.first_ref, f32[16,1024]{1,0:T(8,128)} %constant.24.clone.second_ref, bf16[2048,1024]{1,0:T(8,128)(2,1)} %bitcast.9, ...), custom_call_target="tpu_custom_call", output_to_operand_aliasing={{}: (5, {})} | custom-call | flops 64424509440 | bytes 12582912 | tf_op jit(solution)/shard_map/dft_chunk/pallas_call | solution.py:171
  68.2 6.3 %dft_chunk.6 = f32[32,736,128]{2,1,0:T(8,128)} custom-call(f32[2,32,1024]{2,1,0:T(8,128)} %constant.18.clone.outer_ref.refs_3_, f32[16,1024]{1,0:T(8,128)} %constant.19.clone.first_ref.refs_4_, f32[16,1024]{1,0:T(8,128)} %constant.20.clone.second_ref.refs_5_, bf16[2048,1024]{1,0:T(8,128)(2,1)} %bitcast.10, ...), custom_call_target="tpu_custom_call", output_to_operand_aliasing={{}: (5, {})} | custom-call | flops 24159191040 | bytes 4718592 | tf_op jit(solution)/shard_map/dft_chunk/pallas_call | solution.py:171
  74.5 7.8 %dft_chunk.7 = f32[32,128,128]{2,1,0:T(8,128)} custom-call(f32[2,32,1024]{2,1,0:T(8,128)} %constant.18.clone.outer_ref.refs_3_, f32[8,1024]{1,0:T(8,128)} %constant.25.clone.first_ref, f32[8,1024]{1,0:T(8,128)} %constant.26.clone.second_ref, bf16[2048,1024]{1,0:T(8,128)(2,1)} %bitcast.6, bf16[2048,1024]{1,0:T(8,128)(2,1)} %bitcast.8), custom_call_target="tpu_custom_call" | custom-call | flops 32212254720 | bytes 10485760 | tf_op jit(solution)/shard_map/dft_chunk/pallas_call | solution.py:171
  82.3 5.5 %all-to-all-done.2.refs_0_ = f32[32,160,128]{2,1,0:T(8,128)} async-done(((f32[32,160,128]{2,1,0:T(8,128)}), f32[32,160,128]{2,1,0:T(8,128)}, u32[]{:S(2)}, u32[]{:S(2)}) %all-to-all-start.2) | async-done | bytes 2621472 | tf_op jit(solution)/shard_map/all_to_all | solution.py:451
  87.8 267.3 %all_to_all.15.refs_1_.refs_0_ = f32[32,736,128]{2,1,0:T(8,128)} all-to-all(f32[32,736,128]{2,1,0:T(8,128)} %dft_chunk.6), channel_id=1, replica_groups=mesh['tm'=4,'chan'=8] {'tm','chan'}, dimensions={0} | all-to-all | bytes 24117248 | tf_op jit(solution)/shard_map/all_to_all | solution.py:451
  355.1 2.9 all-to-all-start
  358.0 12.9 %correlate_chunk.4 = (f32[16,2,2,512,512]{4,3,2,1,0:T(8,128)}, f32[8,128]{1,0:T(8,128)}) custom-call(f32[32,160,128]{2,1,0:T(8,128)} %all-to-all-done.2.refs_0_, f32[32,736,128]{2,1,0:T(8,128)} %all_to_all.15.refs_1_.refs_0_), custom_call_target="tpu_custom_call" | custom-call | flops 6442450944 | bytes 20971520 | tf_op jit(solution)/shard_map/correlate_chunk/pallas_call | solution.py:390
  370.9 16.9 %correlate_chunk.5 = (f32[16,2,2,512,512]{4,3,2,1,0:T(8,128)}, f32[8,128]{1,0:T(8,128)}) custom-call(f32[32,736,128]{2,1,0:T(8,128)} %all_to_all.15.refs_1_.refs_0_, f32[16,2,2,512,512]{4,3,2,1,0:T(8,128)} %get-tuple-element.21.refs_1_), custom_call_target="tpu_custom_call", output_to_operand_aliasing={{0}: (1, {})} | custom-call | flops 9663676416 | bytes 31457280 | tf_op jit(solution)/shard_map/correlate_chunk/pallas_call | solution.py:390
  387.8 12.9 %correlate_chunk.6 = (f32[16,2,2,512,512]{4,3,2,1,0:T(8,128)}, f32[8,128]{1,0:T(8,128)}) custom-call(f32[32,736,128]{2,1,0:T(8,128)} %all_to_all.15.refs_1_.refs_0_, f32[16,2,2,512,512]{4,3,2,1,0:T(8,128)} %get-tuple-element.22.refs_1_), custom_call_target="tpu_custom_call", output_to_operand_aliasing={{0}: (1, {})} | custom-call | flops 6442450944 | bytes 20971520 | tf_op jit(solution)/shard_map/correlate_chunk/pallas_call | solution.py:390
  400.7 7.2 %all-to-all-done.refs_0_ = f32[32,128,128]{2,1,0:T(8,128)S(1)} async-done(((f32[32,128,128]{2,1,0:T(8,128)}), f32[32,128,128]{2,1,0:T(8,128)S(1)}, u32[]{:S(2)}, u32[]{:S(2)}) %all-to-all-start) | async-done | bytes 2097184 | tf_op jit(solution)/shard_map/all_to_all | solution.py:451
  407.9 6.0 %correlate_chunk.7 = (f32[16,2,2,512,512]{4,3,2,1,0:T(8,128)}, f32[8,128]{1,0:T(8,128)}) custom-call(f32[32,128,128]{2,1,0:T(8,128)S(1)} %all-to-all-done.refs_0_, f32[16,2,2,512,512]{4,3,2,1,0:T(8,128)} %get-tuple-element.23.refs_1_), custom_call_target="tpu_custom_call", output_to_operand_aliasing={{0}: (1, {})} | custom-call | flops 3221225472 | bytes 10485760 | tf_op jit(solution)/shard_map/correlate_chunk/pallas_call | solution.py:390
Async XLA Ops:
  1.5 24.7 %collective-permute-start = (f32[64,6144]{1,0:T(8,128)S(1)}, f32[64,6144]{1,0:T(8,128)S(1)}, u32[]{:S(2)}, u32[]{:S(2)}) collective-permute-start(f32[64,6144]{1,0:T(8,128)S(1)} %slice.3), channel_id=1, source_target_pairs={{0,8},{8,16},{16,24},{1,9},{9,17},{17,25},{2,10},{10,18},{18,26},{... | collective-permute-start | bytes 4718600 | tf_op jit(solution)/shard_map/ppermute | solution.py:34
  19.1 68.8 %all-to-all-start.2 = ((f32[32,160,128]{2,1,0:T(8,128)}), f32[32,160,128]{2,1,0:T(8,128)}, u32[]{:S(2)}, u32[]{:S(2)}) async-start(f32[32,160,128]{2,1,0:T(8,128)} %first_chunk.1), calls=%async_computation.2 | async-start | bytes 5242880 | tf_op jit(solution)/shard_map/all_to_all | solution.py:451
  26.2 1.1 copy-start
  355.1 52.8 %all-to-all-start = ((f32[32,128,128]{2,1,0:T(8,128)}), f32[32,128,128]{2,1,0:T(8,128)S(1)}, u32[]{:S(2)}, u32[]{:S(2)}) async-start(f32[32,128,128]{2,1,0:T(8,128)} %dft_chunk.7), calls=%async_computation | async-start | bytes 4194304 | tf_op jit(solution)/shard_map/all_to_all | solution.py:451

commit v6 on v5

--- a/solution.py
+++ b/solution.py
@@ -13,7 +13,7 @@
 AXES = ("tm", "chan")
 PAIR = 2
 WIDE = 2
-LATE = 6
+LATE = 10
 NT = (((1,), (1,)), ((), ()))
 NN = (((1,), (0,)), ((), ()))
 
@@ -414,7 +414,7 @@
 def chunk_plan(owned):
     unit = owned // 8
     if owned % 32 == 0:
-        return [[(0, 2 * unit)], [(2 * unit + 1, 3 * unit), (4 * unit, 2 * unit)], [(1, unit)]]
+        return [[(0, 4 * unit)], [(2 * unit + 1, 3 * unit)], [(1, unit)]]
     return [[(parity, owned // 2)] for parity in (0, 1)]
 
 

time: 415 us -> 414 us (level)
  waiting for transfers between devices: 12.7 us -> 27.7 us
  blocking collectives: 267 us -> 256 us
  Pallas kernels: 119 us -> 114 us
    all_to_all x2, waiting for transfers between devices: 12.7 us -> 27.7 us  [exchange(): return lax.all_to_all(value, AXES, split_axis=0, concat_axis=0, tiled=True)]
    all_to_all x1, blocking collectives: 267 us -> 256 us  [exchange(): return lax.all_to_all(value, AXES, split_axis=0, concat_axis=0, tiled=True)]
    pallas_call x4 -> x3, Pallas kernels: 39.2 us -> 34.9 us  [dft_chunk(): pl.pallas_call(functools.partial(dft_kernel, owners, per), grid=(blocks /...]
    pallas_call x4 -> x3, Pallas kernels: 48.7 us -> 49.6 us  [correlate_chunk(): pl.pallas_call(functools.partial(correlate_kernel, sizes, 1.0 / spectra,...]
  transfers between devices with their start and end apart: 3 -> 3, of which waited for: 2 -> 2; matrix products, arithmetic and copies ran while one was open for 0% -> 0% of each run, Pallas kernels for 27% -> 26%
where the time goes in v6:
time: 414 us; the launch traced here: 413 us
  blocking collectives  256 us (62%)
  Pallas kernels  114 us (28%)
  waiting for transfers between devices  27.7 us (7%)
  starting transfers between devices  12.5 us (3%)
    all_to_all x1, blocking collectives, exchange(): return lax.all_to_all(value, AXES, split_axis=0, concat_axis=0, tiled=True)  256 us
    pallas_call x3, Pallas kernels, correlate_chunk(): pl.pallas_call(functools.partial(correlate_kernel, sizes, 1.0 / spectra,...  49.6 us
    pallas_call x3, Pallas kernels, dft_chunk(): pl.pallas_call(functools.partial(dft_kernel, owners, per), grid=(blocks /...  34.9 us
    all_to_all x2, waiting for transfers between devices, exchange(): return lax.all_to_all(value, AXES, split_axis=0, concat_axis=0, tiled=True)  27.7 us
    pallas_call x1, Pallas kernels, filtered_parts(): pl.pallas_call(functools.partial(filter_kernel, blocks, groups, taps), gr...  15.6 us
    pallas_call x1, Pallas kernels, first_chunk(): pl.pallas_call(functools.partial(first_kernel, owners, per, taps, groups)...  14.1 us
    all_to_all x2, starting transfers between devices, exchange(): return lax.all_to_all(value, AXES, split_axis=0, concat_axis=0, tiled=True)  10.1 us
  transfers between devices with their start and end apart: 3, of which 2 were waited for; matrix products, arithmetic and copies ran while one was open for 0% of the time, Pallas kernels for 26%

profile of v6, /device:TPU:0, one launch (start us, length us, event | category | flops | bytes accessed | tf_op | source)
XLA Modules:
  0.0 413.2 jit_solution(14454934043389669963)
XLA Ops:
  0.0 1.5 slice.3
  1.5 2.5 collective-permute-start
  4.0 14.1 %first_chunk.1 = f32[32,192,128]{2,1,0:T(8,128)} custom-call(f32[64,65536]{1,0:T(8,128)} %refs_1_.1, f32[64,65536]{1,0:T(8,128)} %refs_1_.1, f32[4,2048]{1,0:T(4,128)} %refs_2_.1, f32[2,32,1024]{2,1,0:T(8,128)} %constant.14.clone.outer_ref.refs_3_, f32[32,1024]{1,0:T(8,128)} %constant.15.clone.first_ref.refs_4_, f32[32,1024]{1,0:T(8,128)} %constant.16.clone.second_ref.refs_5_), custom_call_target="tpu_custom_call" | custom-call | flops 4831838208 | bytes 16777216 | tf_op jit(solution)/shard_map/first_chunk/pallas_call | solution.py:274
  18.1 7.1 %all-to-all-start.2 = ((f32[32,192,128]{2,1,0:T(8,128)}), f32[32,192,128]{2,1,0:T(8,128)}, u32[]{:S(2)}, u32[]{:S(2)}) async-start(f32[32,192,128]{2,1,0:T(8,128)} %first_chunk.1), calls=%async_computation.2 | async-start | bytes 6291456 | tf_op jit(solution)/shard_map/all_to_all | solution.py:451
  25.2 0.0 collective-permute-done.halo_ref
  25.2 0.0 copy-start
  25.2 1.1 copy-done
  26.4 15.6 %polyphase_filter.1 = (bf16[16,2,64,1024]{3,2,1,0:T(8,128)(2,1)}, bf16[16,2,64,1024]{3,2,1,0:T(8,128)(2,1)}, bf16[16,2,64,1024]{3,2,1,0:T(8,128)(2,1)}, bf16[16,2,64,1024]{3,2,1,0:T(8,128)(2,1)}) custom-call(f32[64,65536]{1,0:T(8,128)} %refs_1_.1, f32[64,6144]{1,0:T(8,128)} %copy-done, f32[4,2048]{1,0:T(4,128)} %refs_2_.1), custom_call_target="tpu_custom_call" | custom-call | flops 33554432000 | bytes 33554432 | tf_op jit(solution)/shard_map/polyphase_filter/pallas_call | solution.py:89
  42.0 7.8 %dft_chunk.5 = f32[32,128,128]{2,1,0:T(8,128)} custom-call(f32[2,32,1024]{2,1,0:T(8,128)} %constant.14.clone.outer_ref.refs_3_, f32[8,1024]{1,0:T(8,128)} %constant.19.clone.first_ref, f32[8,1024]{1,0:T(8,128)} %constant.20.clone.second_ref, bf16[2048,1024]{1,0:T(8,128)(2,1)} %bitcast.7, bf16[2048,1024]{1,0:T(8,128)(2,1)} %bitcast.9), custom_call_target="tpu_custom_call" | custom-call | flops 32212254720 | bytes 10485760 | tf_op jit(solution)/shard_map/dft_chunk/pallas_call | solution.py:171
  49.8 14.3 %dft_chunk.3.rest_0_ = f32[32,704,128]{2,1,0:T(8,128)} custom-call(f32[2,32,1024]{2,1,0:T(8,128)} %constant.14.clone.outer_ref.refs_3_, f32[24,1024]{1,0:T(8,128)} %constant.17.clone.first_ref, f32[24,1024]{1,0:T(8,128)} %constant.18.clone.second_ref, bf16[2048,1024]{1,0:T(8,128)(2,1)} %bitcast.8, bf16[2048,1024]{1,0:T(8,128)(2,1)} %bitcast.10), custom_call_target="tpu_custom_call" | custom-call | flops 96636764160 | bytes 14680064 | tf_op jit(solution)/shard_map/dft_chunk/pallas_call | solution.py:171
  64.1 12.8 %dft_chunk.4 = f32[32,704,128]{2,1,0:T(8,128)} custom-call(f32[2,32,1024]{2,1,0:T(8,128)} %constant.14.clone.outer_ref.refs_3_, f32[32,1024]{1,0:T(8,128)} %constant.15.clone.first_ref.refs_4_, f32[32,1024]{1,0:T(8,128)} %constant.16.clone.second_ref.refs_5_, bf16[2048,1024]{1,0:T(8,128)(2,1)} %bitcast.5, ...), custom_call_target="tpu_custom_call", output_to_operand_aliasing={{}: (5, {})} | custom-call | flops 80530636800 | bytes 10485760 | tf_op jit(solution)/shard_map/dft_chunk/pallas_call | solution.py:171
  76.9 21.4 %all-to-all-done.2.refs_0_ = f32[32,192,128]{2,1,0:T(8,128)} async-done(((f32[32,192,128]{2,1,0:T(8,128)}), f32[32,192,128]{2,1,0:T(8,128)}, u32[]{:S(2)}, u32[]{:S(2)}) %all-to-all-start.2) | async-done | bytes 3145760 | tf_op jit(solution)/shard_map/all_to_all | solution.py:451
  98.3 256.0 %all_to_all.15.refs_1_.refs_0_ = f32[32,704,128]{2,1,0:T(8,128)} all-to-all(f32[32,704,128]{2,1,0:T(8,128)} %dft_chunk.4), channel_id=1, replica_groups=mesh['tm'=4,'chan'=8] {'tm','chan'}, dimensions={0} | all-to-all | bytes 23068672 | tf_op jit(solution)/shard_map/all_to_all | solution.py:451
  354.3 2.9 all-to-all-start
  357.2 26.7 %correlate_chunk.3 = (f32[16,2,2,512,512]{4,3,2,1,0:T(8,128)}, f32[8,128]{1,0:T(8,128)}) custom-call(f32[32,192,128]{2,1,0:T(8,128)} %all-to-all-done.2.refs_0_, f32[32,704,128]{2,1,0:T(8,128)} %all_to_all.15.refs_1_.refs_0_), custom_call_target="tpu_custom_call" | custom-call | flops 12884901888 | bytes 41943040 | tf_op jit(solution)/shard_map/correlate_chunk/pallas_call | solution.py:390
  384.0 16.9 %correlate_chunk.4 = (f32[16,2,2,512,512]{4,3,2,1,0:T(8,128)}, f32[8,128]{1,0:T(8,128)}) custom-call(f32[32,704,128]{2,1,0:T(8,128)} %all_to_all.15.refs_1_.refs_0_, f32[16,2,2,512,512]{4,3,2,1,0:T(8,128)} %get-tuple-element.20.refs_1_), custom_call_target="tpu_custom_call", output_to_operand_aliasing={{0}: (1, {})} | custom-call | flops 9663676416 | bytes 31457280 | tf_op jit(solution)/shard_map/correlate_chunk/pallas_call | solution.py:390
  400.8 6.3 %all-to-all-done.refs_0_ = f32[32,128,128]{2,1,0:T(8,128)S(1)} async-done(((f32[32,128,128]{2,1,0:T(8,128)}), f32[32,128,128]{2,1,0:T(8,128)S(1)}, u32[]{:S(2)}, u32[]{:S(2)}) %all-to-all-start) | async-done | bytes 2097184 | tf_op jit(solution)/shard_map/all_to_all | solution.py:451
  407.1 6.0 %correlate_chunk.5 = (f32[16,2,2,512,512]{4,3,2,1,0:T(8,128)}, f32[8,128]{1,0:T(8,128)}) custom-call(f32[32,128,128]{2,1,0:T(8,128)S(1)} %all-to-all-done.refs_0_, f32[16,2,2,512,512]{4,3,2,1,0:T(8,128)} %get-tuple-element.21.refs_1_), custom_call_target="tpu_custom_call", output_to_operand_aliasing={{0}: (1, {})} | custom-call | flops 3221225472 | bytes 10485760 | tf_op jit(solution)/shard_map/correlate_chunk/pallas_call | solution.py:390
Async XLA Ops:
  1.5 23.7 %collective-permute-start = (f32[64,6144]{1,0:T(8,128)S(1)}, f32[64,6144]{1,0:T(8,128)S(1)}, u32[]{:S(2)}, u32[]{:S(2)}) collective-permute-start(f32[64,6144]{1,0:T(8,128)S(1)} %slice.3), channel_id=1, source_target_pairs={{0,8},{8,16},{16,24},{1,9},{9,17},{17,25},{2,10},{10,18},{18,26},{... | collective-permute-start | bytes 4718600 | tf_op jit(solution)/shard_map/ppermute | solution.py:34
  18.1 80.2 %all-to-all-start.2 = ((f32[32,192,128]{2,1,0:T(8,128)}), f32[32,192,128]{2,1,0:T(8,128)}, u32[]{:S(2)}, u32[]{:S(2)}) async-start(f32[32,192,128]{2,1,0:T(8,128)} %first_chunk.1), calls=%async_computation.2 | async-start | bytes 6291456 | tf_op jit(solution)/shard_map/all_to_all | solution.py:451
  25.2 1.1 copy-start
  354.3 52.8 %all-to-all-start = ((f32[32,128,128]{2,1,0:T(8,128)}), f32[32,128,128]{2,1,0:T(8,128)S(1)}, u32[]{:S(2)}, u32[]{:S(2)}) async-start(f32[32,128,128]{2,1,0:T(8,128)} %dft_chunk.5), calls=%async_computation | async-start | bytes 4194304 | tf_op jit(solution)/shard_map/all_to_all | solution.py:451

commit v7 on v6

--- a/solution.py
+++ b/solution.py
@@ -300,7 +300,7 @@
     )(*([voltages] * groups), fir_taps, outer, first, second)
 
 
-def correlate_kernel(sizes, scale, places, *refs):
+def correlate_kernel(sizes, places, *refs):
     tm_count, chan_count, blocks, per, inputs = sizes
     groups = LANES // inputs
     channels = per // 2
@@ -363,7 +363,7 @@
         high_t, low_t = high.T, low.T
         for which, (other_high, other_low) in enumerate([(high, low), (turned_high, turned_low)]):
             total = dot(high_t, other_high) + dot(high_t, other_low) + dot(low_t, other_high)
-            out_ref[sub, 0, which] = total * scale
+            out_ref[sub, 0, which] = total
 
 
 def correlate_chunk(pieces, held, start, owned, sizes, spectra):
@@ -388,7 +388,7 @@
         operands.append(held)
         in_specs.append(pl.BlockSpec(memory_space=pl.ANY))
     return pl.pallas_call(
-        functools.partial(correlate_kernel, sizes, 1.0 / spectra, places),
+        functools.partial(correlate_kernel, sizes, places),
         grid=(channels // PAIR,),
         in_specs=in_specs,
         out_specs=[
@@ -418,11 +418,11 @@
     return [[(parity, owned // 2)] for parity in (0, 1)]
 
 
-def phases(frame, owners, owned, segments):
+def phases(frame, owners, owned, segments, spectra):
     samples = np.arange(frame // 2)
     outer = 2.0 * np.pi * ((np.arange(owners)[:, None] * owned * samples) % frame) / frame
     outer = np.stack([np.cos(outer), np.sin(outer)]).astype(np.float32)
-    scale = 1.0 / np.sqrt(float(frame))
+    scale = 1.0 / np.sqrt(float(frame * spectra))
     tables = {}
     for start, count in segments:
         channels = start + 2 * np.arange(count)
@@ -444,7 +444,7 @@
     groups = LANES // inputs
     blocks = spec_dev // groups
     chunks = chunk_plan(owned)
-    outer, tables = phases(frame, owners, owned, sum(chunks, []))
+    outer, tables = phases(frame, owners, owned, sum(chunks, []), tm_count * spec_dev)
     split = blocks > LATE and len(chunks) > 2
 
     def exchange(value):

time: 414 us -> 414 us (level)
  no operation moved by 1% of the time
where the time goes in v7:
time: 414 us; the launch traced here: 413 us
  blocking collectives  256 us (62%)
  Pallas kernels  114 us (28%)
  waiting for transfers between devices  27.8 us (7%)
  starting transfers between devices  12.5 us (3%)
    all_to_all x1, blocking collectives, exchange(): return lax.all_to_all(value, AXES, split_axis=0, concat_axis=0, tiled=True)  256 us
    pallas_call x3, Pallas kernels, correlate_chunk(): pl.pallas_call(functools.partial(correlate_kernel, sizes, places), grid=(...  49.5 us
    pallas_call x3, Pallas kernels, dft_chunk(): pl.pallas_call(functools.partial(dft_kernel, owners, per), grid=(blocks /...  34.9 us
    all_to_all x2, waiting for transfers between devices, exchange(): return lax.all_to_all(value, AXES, split_axis=0, concat_axis=0, tiled=True)  27.7 us
    pallas_call x1, Pallas kernels, filtered_parts(): pl.pallas_call(functools.partial(filter_kernel, blocks, groups, taps), gr...  15.6 us
    pallas_call x1, Pallas kernels, first_chunk(): pl.pallas_call(functools.partial(first_kernel, owners, per, taps, groups)...  14.1 us
    all_to_all x2, starting transfers between devices, exchange(): return lax.all_to_all(value, AXES, split_axis=0, concat_axis=0, tiled=True)  10.1 us
  transfers between devices with their start and end apart: 3, of which 2 were waited for; matrix products, arithmetic and copies ran while one was open for 0% of the time, Pallas kernels for 26%

profile of v7, /device:TPU:0, one launch (start us, length us, event | category | flops | bytes accessed | tf_op | source)
XLA Modules:
  0.0 413.1 jit_solution(13456255614538007109)
XLA Ops:
  0.0 1.5 slice.3
  1.5 2.5 collective-permute-start
  4.0 14.1 %first_chunk.1 = f32[32,192,128]{2,1,0:T(8,128)} custom-call(f32[64,65536]{1,0:T(8,128)} %refs_1_.1, f32[64,65536]{1,0:T(8,128)} %refs_1_.1, f32[4,2048]{1,0:T(4,128)} %refs_2_.1, f32[2,32,1024]{2,1,0:T(8,128)} %constant.14.clone.outer_ref.refs_3_, f32[32,1024]{1,0:T(8,128)} %constant.15.clone.first_ref.refs_4_, f32[32,1024]{1,0:T(8,128)} %constant.16.clone.second_ref.refs_5_), custom_call_target="tpu_custom_call" | custom-call | flops 4831838208 | bytes 16777216 | tf_op jit(solution)/shard_map/first_chunk/pallas_call | solution.py:274
  18.1 7.1 %all-to-all-start.2 = ((f32[32,192,128]{2,1,0:T(8,128)}), f32[32,192,128]{2,1,0:T(8,128)}, u32[]{:S(2)}, u32[]{:S(2)}) async-start(f32[32,192,128]{2,1,0:T(8,128)} %first_chunk.1), calls=%async_computation.2 | async-start | bytes 6291456 | tf_op jit(solution)/shard_map/all_to_all | solution.py:451
  25.2 0.0 collective-permute-done.halo_ref
  25.2 0.0 copy-start
  25.2 1.1 copy-done
  26.4 15.6 %polyphase_filter.1 = (bf16[16,2,64,1024]{3,2,1,0:T(8,128)(2,1)}, bf16[16,2,64,1024]{3,2,1,0:T(8,128)(2,1)}, bf16[16,2,64,1024]{3,2,1,0:T(8,128)(2,1)}, bf16[16,2,64,1024]{3,2,1,0:T(8,128)(2,1)}) custom-call(f32[64,65536]{1,0:T(8,128)} %refs_1_.1, f32[64,6144]{1,0:T(8,128)} %copy-done, f32[4,2048]{1,0:T(4,128)} %refs_2_.1), custom_call_target="tpu_custom_call" | custom-call | flops 33554432000 | bytes 33554432 | tf_op jit(solution)/shard_map/polyphase_filter/pallas_call | solution.py:89
  42.0 7.8 %dft_chunk.5 = f32[32,128,128]{2,1,0:T(8,128)} custom-call(f32[2,32,1024]{2,1,0:T(8,128)} %constant.14.clone.outer_ref.refs_3_, f32[8,1024]{1,0:T(8,128)} %constant.19.clone.first_ref, f32[8,1024]{1,0:T(8,128)} %constant.20.clone.second_ref, bf16[2048,1024]{1,0:T(8,128)(2,1)} %bitcast.7, bf16[2048,1024]{1,0:T(8,128)(2,1)} %bitcast.9), custom_call_target="tpu_custom_call" | custom-call | flops 32212254720 | bytes 10485760 | tf_op jit(solution)/shard_map/dft_chunk/pallas_call | solution.py:171
  49.8 14.3 %dft_chunk.3.rest_0_ = f32[32,704,128]{2,1,0:T(8,128)} custom-call(f32[2,32,1024]{2,1,0:T(8,128)} %constant.14.clone.outer_ref.refs_3_, f32[24,1024]{1,0:T(8,128)} %constant.17.clone.first_ref, f32[24,1024]{1,0:T(8,128)} %constant.18.clone.second_ref, bf16[2048,1024]{1,0:T(8,128)(2,1)} %bitcast.8, bf16[2048,1024]{1,0:T(8,128)(2,1)} %bitcast.10), custom_call_target="tpu_custom_call" | custom-call | flops 96636764160 | bytes 14680064 | tf_op jit(solution)/shard_map/dft_chunk/pallas_call | solution.py:171
  64.1 12.8 %dft_chunk.4 = f32[32,704,128]{2,1,0:T(8,128)} custom-call(f32[2,32,1024]{2,1,0:T(8,128)} %constant.14.clone.outer_ref.refs_3_, f32[32,1024]{1,0:T(8,128)} %constant.15.clone.first_ref.refs_4_, f32[32,1024]{1,0:T(8,128)} %constant.16.clone.second_ref.refs_5_, bf16[2048,1024]{1,0:T(8,128)(2,1)} %bitcast.5, ...), custom_call_target="tpu_custom_call", output_to_operand_aliasing={{}: (5, {})} | custom-call | flops 80530636800 | bytes 10485760 | tf_op jit(solution)/shard_map/dft_chunk/pallas_call | solution.py:171
  76.9 21.4 %all-to-all-done.2.refs_0_ = f32[32,192,128]{2,1,0:T(8,128)} async-done(((f32[32,192,128]{2,1,0:T(8,128)}), f32[32,192,128]{2,1,0:T(8,128)}, u32[]{:S(2)}, u32[]{:S(2)}) %all-to-all-start.2) | async-done | bytes 3145760 | tf_op jit(solution)/shard_map/all_to_all | solution.py:451
  98.3 256.0 %all_to_all.15.refs_1_.refs_0_ = f32[32,704,128]{2,1,0:T(8,128)} all-to-all(f32[32,704,128]{2,1,0:T(8,128)} %dft_chunk.4), channel_id=1, replica_groups=mesh['tm'=4,'chan'=8] {'tm','chan'}, dimensions={0} | all-to-all | bytes 23068672 | tf_op jit(solution)/shard_map/all_to_all | solution.py:451
  354.3 2.9 all-to-all-start
  357.2 26.7 %correlate_chunk.3 = (f32[16,2,2,512,512]{4,3,2,1,0:T(8,128)}, f32[8,128]{1,0:T(8,128)}) custom-call(f32[32,192,128]{2,1,0:T(8,128)} %all-to-all-done.2.refs_0_, f32[32,704,128]{2,1,0:T(8,128)} %all_to_all.15.refs_1_.refs_0_), custom_call_target="tpu_custom_call" | custom-call | flops 12884901888 | bytes 41943040 | tf_op jit(solution)/shard_map/correlate_chunk/pallas_call | solution.py:390
  384.0 16.8 %correlate_chunk.4 = (f32[16,2,2,512,512]{4,3,2,1,0:T(8,128)}, f32[8,128]{1,0:T(8,128)}) custom-call(f32[32,704,128]{2,1,0:T(8,128)} %all_to_all.15.refs_1_.refs_0_, f32[16,2,2,512,512]{4,3,2,1,0:T(8,128)} %get-tuple-element.20.refs_1_), custom_call_target="tpu_custom_call", output_to_operand_aliasing={{0}: (1, {})} | custom-call | flops 9663676416 | bytes 31457280 | tf_op jit(solution)/shard_map/correlate_chunk/pallas_call | solution.py:390
  400.8 6.4 %all-to-all-done.refs_0_ = f32[32,128,128]{2,1,0:T(8,128)S(1)} async-done(((f32[32,128,128]{2,1,0:T(8,128)}), f32[32,128,128]{2,1,0:T(8,128)S(1)}, u32[]{:S(2)}, u32[]{:S(2)}) %all-to-all-start) | async-done | bytes 2097184 | tf_op jit(solution)/shard_map/all_to_all | solution.py:451
  407.1 6.0 %correlate_chunk.5 = (f32[16,2,2,512,512]{4,3,2,1,0:T(8,128)}, f32[8,128]{1,0:T(8,128)}) custom-call(f32[32,128,128]{2,1,0:T(8,128)S(1)} %all-to-all-done.refs_0_, f32[16,2,2,512,512]{4,3,2,1,0:T(8,128)} %get-tuple-element.21.refs_1_), custom_call_target="tpu_custom_call", output_to_operand_aliasing={{0}: (1, {})} | custom-call | flops 3221225472 | bytes 10485760 | tf_op jit(solution)/shard_map/correlate_chunk/pallas_call | solution.py:390
Async XLA Ops:
  1.5 23.7 %collective-permute-start = (f32[64,6144]{1,0:T(8,128)S(1)}, f32[64,6144]{1,0:T(8,128)S(1)}, u32[]{:S(2)}, u32[]{:S(2)}) collective-permute-start(f32[64,6144]{1,0:T(8,128)S(1)} %slice.3), channel_id=1, source_target_pairs={{0,8},{8,16},{16,24},{1,9},{9,17},{17,25},{2,10},{10,18},{18,26},{... | collective-permute-start | bytes 4718600 | tf_op jit(solution)/shard_map/ppermute | solution.py:34
  18.1 80.2 %all-to-all-start.2 = ((f32[32,192,128]{2,1,0:T(8,128)}), f32[32,192,128]{2,1,0:T(8,128)}, u32[]{:S(2)}, u32[]{:S(2)}) async-start(f32[32,192,128]{2,1,0:T(8,128)} %first_chunk.1), calls=%async_computation.2 | async-start | bytes 6291456 | tf_op jit(solution)/shard_map/all_to_all | solution.py:451
  25.2 1.1 copy-start
  354.3 52.8 %all-to-all-start = ((f32[32,128,128]{2,1,0:T(8,128)}), f32[32,128,128]{2,1,0:T(8,128)S(1)}, u32[]{:S(2)}, u32[]{:S(2)}) async-start(f32[32,128,128]{2,1,0:T(8,128)} %dft_chunk.5), calls=%async_computation | async-start | bytes 4194304 | tf_op jit(solution)/shard_map/all_to_all | solution.py:451
